TPU v7x, 512 devices: a whole 4x4x16 slice. The times are simulated.
512 devices in a mesh: wide: 64 (over z, y_lo, core), narrow: 8 (over y_hi, x).
Axes of the slice: x: 4, y: 4 (y_hi: 2, y_lo: 2; y = y_hi * 2 + y_lo), z: 16, core: 2. Of those that a mesh axis runs over, the one named last changes fastest.
Arguments:
- heat_source: float32 [512, 256, 128], P('wide', 'narrow'), may hold values from -8 to 8
- conductivity: float32 [512, 256, 128], P('wide', 'narrow'), may hold values from 0.2 to 5
Outputs:
- solution: float32 [512, 256, 128], P('wide', 'narrow')
All inputs are finite; a program needn't handle non-finite values.
Results may differ from a plain program's by a relative error of at most 0.0049.
Values sent between devices are 32-bit elements; how exact they have to be, the bound alone decides.
A program may use at most 64 MiB of HBM per device.

v0:
```python
import jax
import jax.numpy as jnp
from jax import lax
from jax.sharding import PartitionSpec as P

DEGREE = 3
CITERS = 4


mass_shift = 0.002
cheb_low = 0.25
cheb_high = 2.0


def padded_2(block, sides, width):
    for axis, dim in sides:
        count = lax.axis_size(axis)
        forward = [(i, i + 1) for i in range(count - 1)]
        backward = [(target, source) for source, target in forward]
        low = lax.ppermute(
            lax.slice_in_dim(block, block.shape[dim] - width, None, axis=dim), axis, forward
        )
        high = lax.ppermute(lax.slice_in_dim(block, 0, width, axis=dim), axis, backward)
        block = jnp.concatenate([low, block, high], axis=dim)
    return block


def extend(field):
    padded = padded_2(field, (("wide", 0), ("narrow", 1)), 1)
    return jnp.pad(padded, ((0, 0), (0, 0), (1, 1)))


def level_ops(cond_grid, level_scale, extend_fn):
    padded_cond = extend_fn(cond_grid)
    center = padded_cond[1:-1, 1:-1, 1:-1]
    face_coef = [
        0.5 * (center + padded_cond[2:, 1:-1, 1:-1]),
        0.5 * (center + padded_cond[:-2, 1:-1, 1:-1]),
        0.5 * (center + padded_cond[1:-1, 2:, 1:-1]),
        0.5 * (center + padded_cond[1:-1, :-2, 1:-1]),
        0.5 * (center + padded_cond[1:-1, 1:-1, 2:]),
        0.5 * (center + padded_cond[1:-1, 1:-1, :-2]),
    ]
    coef_total = (
        face_coef[0] + face_coef[1] + face_coef[2] + face_coef[3] + face_coef[4] + face_coef[5]
    )
    diagonal = mass_shift + level_scale * coef_total

    def operate(field):
        padded = extend_fn(field)
        beside = face_coef[0] * padded[2:, 1:-1, 1:-1] + face_coef[1] * padded[:-2, 1:-1, 1:-1]
        beside = (
            beside + face_coef[2] * padded[1:-1, 2:, 1:-1] + face_coef[3] * padded[1:-1, :-2, 1:-1]
        )
        beside = (
            beside + face_coef[4] * padded[1:-1, 1:-1, 2:] + face_coef[5] * padded[1:-1, 1:-1, :-2]
        )
        return diagonal * field - level_scale * beside

    return (operate, diagonal)


def restrict(field):
    size_x, size_y, size_z = field.shape
    return field.reshape(size_x // 2, 2, size_y // 2, 2, size_z // 2, 2).mean(axis=(1, 3, 5))


def prolong(field):
    size_x, size_y, size_z = field.shape
    wider = jnp.broadcast_to(field[:, None, :, None, :, None], (size_x, 2, size_y, 2, size_z, 2))
    return wider.reshape(2 * size_x, 2 * size_y, 2 * size_z)


def smooth(operate, diagonal, source, iterate, inside=None):
    midpoint = 0.5 * (cheb_high + cheb_low)
    half_width = 0.5 * (cheb_high - cheb_low)
    sigma_one = midpoint / half_width
    damping = 1.0 / sigma_one
    if iterate is None:
        scaled = source / diagonal
        iterate = jnp.zeros_like(source)
    else:
        scaled = (source - operate(iterate)) / diagonal
    update = scaled / midpoint
    iterate = iterate + update
    for turn_index in range(DEGREE - 1):
        damp_next = 1.0 / (2.0 * sigma_one - damping)
        scaled = (source - operate(iterate)) / diagonal
        update = damp_next * damping * update + 2.0 * damp_next / half_width * scaled
        iterate = iterate + update
        damping = damp_next
    return iterate


def coarse_solve(operate, diagonal, source, total_curve, total_norm):
    iterate = jnp.zeros_like(source)
    residual = source
    scaled = residual / diagonal
    direction = scaled
    inner_now = total_norm(jnp.sum(residual * scaled))
    for turn_index in range(CITERS):
        image = operate(direction)
        step_size = inner_now / total_curve(jnp.sum(direction * image))
        iterate = iterate + step_size * direction
        residual = residual - step_size * image
        if turn_index + 1 < CITERS:
            scaled = residual / diagonal
            inner_next = total_norm(jnp.sum(residual * scaled))
            direction = scaled + inner_next / inner_now * direction
            inner_now = inner_next
    return iterate


def body(heat_source, conductivity):
    cond_one = restrict(conductivity)
    cond_two = restrict(cond_one)
    op_zero, diag_zero = level_ops(conductivity, 1.0, extend)
    op_one, diag_one = level_ops(cond_one, 0.25, extend)
    fine_iter = smooth(op_zero, diag_zero, heat_source, None)
    src_one = restrict(heat_source - op_zero(fine_iter))
    mid_iter = smooth(op_one, diag_one, src_one, None)
    src_two = restrict(src_one - op_one(mid_iter))
    op_two, diag_two = level_ops(cond_two, 1.0 / 16.0, extend)
    coarse_iter = coarse_solve(
        op_two,
        diag_two,
        src_two,
        lambda value: lax.psum(value, ("wide", "narrow")),
        lambda value: lax.psum(value, ("wide", "narrow")),
    )
    mid_iter = smooth(op_one, diag_one, src_one, mid_iter + prolong(coarse_iter))
    return smooth(op_zero, diag_zero, heat_source, fine_iter + prolong(mid_iter))


def solution(mesh):
    placed = (P("wide", "narrow", None), P("wide", "narrow", None))
    return jax.shard_map(
        body, mesh=mesh, in_specs=placed, out_specs=P("wide", "narrow", None), check_vma=False
    )
```

profile of v0, /device:TPU:1, one launch (start us, length us, event | category | flops | bytes accessed | tf_op | source)
XLA Modules:
  0.0 1132.5 jit_solution(17033380129712585564)
XLA Ops:
  0.7 4.6 collective-permute-start.1
  5.3 5.5 collective-permute-start
  14.8 3.1 collective-permute-done.2
  19.4 3.4 collective-permute-start.5
  24.7 3.1 collective-permute-done.4
  27.8 3.1 collective-permute-start.7
  32.4 10.5 reshape.22
  42.9 4.0 reduce_sum.109
  51.9 4.5 collective-permute-done.8
  56.4 4.5 collective-permute-start.11
  64.2 3.6 collective-permute-start.17
  69.7 3.1 collective-permute-start.13
  74.7 6.6 collective-permute-start.19
  82.6 4.3 collective-permute-start.15
  88.4 5.6 collective-permute-done.14
  94.3 9.8 reshape.21
  104.1 4.0 reduce_sum.108
  108.2 5.0 collective-permute-start.21
  115.2 3.0 collective-permute-done.20
  118.2 6.9 collective-permute-start.23
  127.7 5.7 collective-permute-done.22
  133.6 3.9 collective-permute-start.25
  139.5 3.4 collective-permute-done.24
  142.9 7.3 collective-permute-start.27
  153.4 3.6 collective-permute-start.33
  157.3 4.0 collective-permute-start.29
  163.3 4.3 collective-permute-start.35
  168.9 5.9 collective-permute-start.31
  180.6 6.2 collective-permute-start.37
  188.8 3.0 collective-permute-done.36
  191.8 5.2 collective-permute-start.39
  198.4 6.9 collective-permute-done.38
  206.1 129.8 %all-reduce.19 = (f32[]{:T(128)}, f32[]{:T(128)}) all-reduce(f32[]{:T(128)} %get-tuple-element.6, f32[]{:T(128)} %get-tuple-element.5), channel_id=1, replica_groups=mesh['wide'=64,'narrow'=8] {'wide','narrow'}, use_global_device_ids=true, to_apply=%region_5.6 | all-reduce | flops 2 | bytes 16 | tf_op jit(solution)/shard_map/psum | solution.py:129
  337.8 98.6 %psum.58 = f32[]{:T(128)} all-reduce(f32[]{:T(128)} %get-tuple-element.24), channel_id=1, replica_groups=mesh['wide'=64,'narrow'=8] {'wide','narrow'}, use_global_device_ids=true, to_apply=%region_9.10 | all-reduce | flops 1 | bytes 8 | tf_op jit(solution)/shard_map/psum | solution.py:129
  448.4 3.0 collective-permute-done.42
  452.2 108.4 %psum.59 = f32[]{:T(128)} all-reduce(f32[]{:T(128)} %get-tuple-element.22), channel_id=1, replica_groups=mesh['wide'=64,'narrow'=8] {'wide','narrow'}, use_global_device_ids=true, to_apply=%region_11.12 | all-reduce | flops 1 | bytes 8 | tf_op jit(solution)/shard_map/psum | solution.py:128
  562.6 98.4 %psum.60 = f32[]{:T(128)} all-reduce(f32[]{:T(128)} %get-tuple-element.19), channel_id=1, replica_groups=mesh['wide'=64,'narrow'=8] {'wide','narrow'}, use_global_device_ids=true, to_apply=%region_13.14 | all-reduce | flops 1 | bytes 8 | tf_op jit(solution)/shard_map/psum | solution.py:129
  672.7 3.2 collective-permute-done.46
  676.8 108.3 %psum.61 = f32[]{:T(128)} all-reduce(f32[]{:T(128)} %get-tuple-element.17), channel_id=1, replica_groups=mesh['wide'=64,'narrow'=8] {'wide','narrow'}, use_global_device_ids=true, to_apply=%region_15.16 | all-reduce | flops 1 | bytes 8 | tf_op jit(solution)/shard_map/psum | solution.py:128
  786.9 98.6 %psum.62 = f32[]{:T(128)} all-reduce(f32[]{:T(128)} %multiply_reduce_fusion), channel_id=1, replica_groups=mesh['wide'=64,'narrow'=8] {'wide','narrow'}, use_global_device_ids=true, to_apply=%region_17.18 | all-reduce | flops 1 | bytes 8 | tf_op jit(solution)/shard_map/psum | solution.py:129
  897.4 3.2 collective-permute-done.50
  901.4 108.2 %psum.63 = f32[]{:T(128)} all-reduce(f32[]{:T(128)} %fusion.201), channel_id=1, replica_groups=mesh['wide'=64,'narrow'=8] {'wide','narrow'}, use_global_device_ids=true, to_apply=%region_19.20 | all-reduce | flops 1 | bytes 8 | tf_op jit(solution)/shard_map/psum | solution.py:128
  1022.5 3.0 collective-permute-done.54
  1025.7 3.4 collective-permute-start.57
  1031.0 3.0 collective-permute-done.56
  1038.2 3.5 collective-permute-done.58
  1042.0 3.6 collective-permute-start.61
  1047.5 3.4 collective-permute-done.60
  1051.0 7.3 collective-permute-start.63
  1059.5 3.0 collective-permute-done.62
  1062.8 3.9 broadcast_in_dim.5
  1066.7 6.9 reshape.25
  1073.7 3.9 collective-permute-start.65
  1079.5 3.5 collective-permute-done.64
  1083.0 5.2 collective-permute-start.67
  1089.6 3.1 collective-permute-done.66
  1093.1 3.8 collective-permute-start.69
  1098.8 3.6 collective-permute-done.68
  1102.4 5.2 collective-permute-start.71
  1109.0 3.1 collective-permute-done.70
  1112.5 3.8 collective-permute-start.73
  1118.2 3.6 collective-permute-done.72
  1121.8 5.2 collective-permute-start.75
  1128.4 3.1 collective-permute-done.74
  (201 shorter events, 116.4 us)
Async XLA Ops:
  0.7 10.1 collective-permute-start.1
  5.3 6.4 collective-permute-start
  19.4 5.3 collective-permute-start.5
  22.7 5.1 collective-permute-start.4
  27.8 19.1 %collective-permute-start.7 = (f32[10,1,128]{2,1,0:T(1,128)S(1)}, f32[10,1,128]{2,1,0:T(1,128)S(1)}, u32[]{:S(2)}, u32[]{:S(2)}) collective-permute-start(f32[10,1,128]{2,1,0:T(1,128)S(1)} %get-tuple-element.59), channel_id=1, source_target_pairs={{0,1},{1,2},{2,3},{3,4},{4,5},{5,6},{6,7},{8,9},{9,10},{10,11},{11... | collective-permute-start | bytes 15368 | tf_op jit(solution)/shard_map/ppermute | solution.py:20
  31.0 16.0 %collective-permute-start.6 = (f32[10,1,128]{2,1,0:T(1,128)S(1)}, f32[10,1,128]{2,1,0:T(1,128)S(1)}, u32[]{:S(2)}, u32[]{:S(2)}) collective-permute-start(f32[10,1,128]{2,1,0:T(1,128)S(1)} %get-tuple-element.60), channel_id=1, source_target_pairs={{1,0},{2,1},{3,2},{4,3},{5,4},{6,5},{7,6},{9,8},{10,9},{11,10},{12... | collective-permute-start | bytes 15368 | tf_op jit(solution)/shard_map/ppermute | solution.py:23
  47.4 4.5 collective-permute-start.9
  50.0 6.4 collective-permute-start.8
  56.4 11.4 %collective-permute-start.11 = (f32[10,1,128]{2,1,0:T(1,128)S(1)}, f32[10,1,128]{2,1,0:T(1,128)S(1)}, u32[]{:S(2)}, u32[]{:S(2)}) collective-permute-start(f32[10,1,128]{2,1,0:T(1,128)S(1)} %get-tuple-element.57), channel_id=1, source_target_pairs={{0,1},{1,2},{2,3},{3,4},{4,5},{5,6},{6,7},{8,9},{9,10},{10,11},{11... | collective-permute-start | bytes 15368 | tf_op jit(solution)/shard_map/ppermute | solution.py:20
  61.0 8.3 collective-permute-start.10
  62.3 12.4 %collective-permute-start.16 = (f32[1,16,64]{2,1,0:T(8,128)S(1)}, f32[1,16,64]{2,1,0:T(8,128)S(1)}, u32[]{:S(2)}, u32[]{:S(2)}) collective-permute-start(f32[1,16,64]{2,1,0:T(8,128)S(1)} %get-tuple-element.103), channel_id=1, source_target_pairs={{8,0},{16,8},{24,16},{32,24},{40,32},{48,40},{56,48},{64,56},{72,6... | collective-permute-start | bytes 12296 | tf_op jit(solution)/shard_map/ppermute | solution.py:23
  64.2 10.5 collective-permute-start.17
  69.7 12.9 %collective-permute-start.13 = (f32[1,32,128]{2,1,0:T(8,128)S(1)}, f32[1,32,128]{2,1,0:T(8,128)S(1)}, u32[]{:S(2)}, u32[]{:S(2)}) collective-permute-start(f32[1,32,128]{2,1,0:T(8,128)S(1)} %get-tuple-element.69), channel_id=1, source_target_pairs={{0,8},{8,16},{16,24},{24,32},{32,40},{40,48},{48,56},{56,64},{64,7... | collective-permute-start | bytes 49160 | tf_op jit(solution)/shard_map/ppermute | solution.py:20
  72.8 9.9 collective-permute-start.12
  74.7 13.5 %collective-permute-start.19 = (f32[6,1,64]{2,1,0:T(1,128)S(1)}, f32[6,1,64]{2,1,0:T(1,128)S(1)}, u32[]{:S(2)}, u32[]{:S(2)}) collective-permute-start(f32[6,1,64]{2,1,0:T(1,128)S(1)} %get-tuple-element.89), channel_id=1, source_target_pairs={{0,1},{1,2},{2,3},{3,4},{4,5},{5,6},{6,7},{8,9},{9,10},{10,11},{11... | collective-permute-start | bytes 4616 | tf_op jit(solution)/shard_map/ppermute | solution.py:20
  81.3 6.9 collective-permute-start.18
  82.6 5.7 collective-permute-start.15
  86.9 7.0 collective-permute-start.14
  108.2 6.9 collective-permute-start.21
  113.3 5.0 collective-permute-start.20
  118.2 9.4 collective-permute-start.23
  125.1 8.2 collective-permute-start.22
  133.6 5.9 collective-permute-start.25
  137.5 5.4 collective-permute-start.24
  142.9 14.2 %collective-permute-start.27 = (f32[6,1,64]{2,1,0:T(1,128)S(1)}, f32[6,1,64]{2,1,0:T(1,128)S(1)}, u32[]{:S(2)}, u32[]{:S(2)}) collective-permute-start(f32[6,1,64]{2,1,0:T(1,128)S(1)} %get-tuple-element.85), channel_id=1, source_target_pairs={{0,1},{1,2},{2,3},{3,4},{4,5},{5,6},{6,7},{8,9},{9,10},{10,11},{11... | collective-permute-start | bytes 4616 | tf_op jit(solution)/shard_map/ppermute | solution.py:20
  150.2 6.9 collective-permute-start.26
  151.5 11.7 %collective-permute-start.32 = (f32[1,8,32]{2,1,0:T(8,128)S(1)}, f32[1,8,32]{2,1,0:T(8,128)S(1)}, u32[]{:S(2)}, u32[]{:S(2)}) collective-permute-start(f32[1,8,32]{2,1,0:T(8,128)S(1)} %get-tuple-element.123), channel_id=1, source_target_pairs={{8,0},{16,8},{24,16},{32,24},{40,32},{48,40},{56,48},{64,56},{72,6... | collective-permute-start | bytes 3080 | tf_op jit(solution)/shard_map/ppermute | solution.py:23
  153.4 9.8 collective-permute-start.33
  157.3 11.5 %collective-permute-start.29 = (f32[1,16,64]{2,1,0:T(8,128)S(1)}, f32[1,16,64]{2,1,0:T(8,128)S(1)}, u32[]{:S(2)}, u32[]{:S(2)}) collective-permute-start(f32[1,16,64]{2,1,0:T(8,128)S(1)} %get-tuple-element.97), channel_id=1, source_target_pairs={{0,8},{8,16},{16,24},{24,32},{32,40},{40,48},{48,56},{56,64},{64,7... | collective-permute-start | bytes 12296 | tf_op jit(solution)/shard_map/ppermute | solution.py:20
  161.3 7.6 collective-permute-start.28
  163.3 12.8 %collective-permute-start.35 = (f32[4,1,32]{2,1,0:T(1,128)S(1)}, f32[4,1,32]{2,1,0:T(1,128)S(1)}, u32[]{:S(2)}, u32[]{:S(2)}) collective-permute-start(f32[4,1,32]{2,1,0:T(1,128)S(1)} %get-tuple-element.113), channel_id=1, source_target_pairs={{0,1},{1,2},{2,3},{3,4},{4,5},{5,6},{6,7},{8,9},{9,10},{10,11},{11... | collective-permute-start | bytes 1544 | tf_op jit(solution)/shard_map/ppermute | solution.py:20
  167.5 8.5 collective-permute-start.34
  168.9 7.3 collective-permute-start.31
  180.6 8.2 collective-permute-start.37
  186.9 4.9 collective-permute-start.36
  191.8 6.6 collective-permute-start.39
  197.1 8.2 collective-permute-start.38
  437.7 4.6 collective-permute-start.41
  440.4 4.9 collective-permute-start.40
  662.3 4.7 collective-permute-start.45
  665.1 4.9 collective-permute-start.44
  671.4 4.6 collective-permute-start.46
  886.8 4.9 collective-permute-start.49
  889.7 4.9 collective-permute-start.48
  896.1 4.6 collective-permute-start.50
  1013.8 5.0 collective-permute-start.52
  1025.7 5.3 collective-permute-start.57
  1029.1 5.0 collective-permute-start.56
  1036.9 4.9 collective-permute-start.58
  1042.0 5.5 collective-permute-start.61
  1045.6 5.4 collective-permute-start.60
  1051.0 8.6 collective-permute-start.63
  1073.7 5.8 collective-permute-start.65
  1077.5 5.5 collective-permute-start.64
  1083.0 6.6 collective-permute-start.67
  1088.3 4.4 collective-permute-start.66
  1093.1 5.7 collective-permute-start.69
  1096.9 5.6 collective-permute-start.68
  1102.4 6.6 collective-permute-start.71
  1107.7 4.4 collective-permute-start.70
  1112.5 5.7 collective-permute-start.73
  1116.3 5.6 collective-permute-start.72
  1121.8 6.6 collective-permute-start.75
  1127.1 4.4 collective-permute-start.74
  (14 other events, 77.9 us)
where the time goes:
time: 1150 us; the launch traced here: 1130 us
  blocking collectives  750 us (65%)
  starting transfers between devices  216 us (19%)
  waiting for transfers between devices  99.8 us (9%)
  local copies, waits for them, and re-layouts  35.9 us (3%)
  other arithmetic  19.7 us (2%)
    psum x7, blocking collectives, body(): lax.psum(value, ('wide', 'narrow'))  750 us
    ppermute x38, starting transfers between devices, padded_2(): lax.ppermute(lax.slice_in_dim(block, block.shape[dim] - width, None, axis...  151 us
    ppermute x38, waiting for transfers between devices, padded_2(): lax.ppermute(lax.slice_in_dim(block, 0, width, axis=dim), axis, backward)  99.7 us
    ppermute x38, starting transfers between devices, padded_2(): lax.ppermute(lax.slice_in_dim(block, 0, width, axis=dim), axis, backward)  65.2 us
  transfers between devices with their start and end apart: 76, of which 29 were waited for; matrix products, arithmetic and copies ran while one was open for 2% of the time, Pallas kernels for 0%

commit v1 on v0

v1 whole, which is shorter than its diff:
```python
import functools
import jax
import jax.numpy as jnp
from jax import lax
from jax.experimental import pallas as pl
from jax.experimental.pallas import tpu as pltpu
from jax.sharding import PartitionSpec as P

MASS = 0.002
LOW, HIGH = 0.25, 2.0
THETA = 0.5 * (HIGH + LOW)
DELTA = 0.5 * (HIGH - LOW)
SIGMA = THETA / DELTA
RHO1 = 1.0 / SIGMA
RHO2 = 1.0 / (2.0 * SIGMA - RHO1)
RHO3 = 1.0 / (2.0 * SIGMA - RHO2)
KEEP1, GAIN1 = RHO2 * RHO1, 2.0 * RHO2 / DELTA
KEEP2, GAIN2 = RHO3 * RHO2, 2.0 * RHO3 / DELTA
F32 = jnp.float32
LANES = 128
MESH = pl.DeviceIdType.MESH


class Level:
    def __init__(self, planes, first, own, rows, own_rows, repeat, scale):
        self.planes, self.first, self.own = planes, first, own
        self.rows, self.own_rows, self.repeat, self.scale = rows, own_rows, repeat, scale


FINE = Level(16, 4, 8, 48, 32, 1, 1.0)
MID = Level(20, 8, 4, 32, 16, 2, 0.25)
COARSE = Level(14, 6, 2, 24, 8, 4, 1.0 / 16.0)

FIELDS = ("k", "raw", "cx", "cyu", "cyd", "czr", "czl", "inv", "diag", "src", "hat", "upd", "it")


def planes(lo, hi, fn, unroll=2):
    count = hi - lo
    while count % unroll:
        unroll -= 1

    def step(i, carry):
        for k in range(unroll):
            fn(lo + i * unroll + k)
        return carry

    lax.fori_loop(0, count // unroll, step, 0)


def roll_rows(x, by):
    return pltpu.roll(x, by % x.shape[0], 0)


def roll_lanes(x, by):
    return pltpu.roll(x, by % LANES, 1)


def lane_of(rows):
    return lax.broadcasted_iota(jnp.int32, (rows, LANES), 1)


def row_of(rows):
    return lax.broadcasted_iota(jnp.int32, (rows, LANES), 0)


def near_sum(lv, f, ref, p, centers):
    cxu, cxd = f["cx"][p], f["cx"][p - 1]
    cyu, cyd, czr, czl = f["cyu"][p], f["cyd"][p], f["czr"][p], f["czl"][p]
    sums = []
    for v, c in enumerate(centers):
        at = ref.at[v] if len(ref.shape) == 4 else ref
        sums.append(
            cxu * at[p + 1]
            + cxd * at[p - 1]
            + cyu * roll_rows(c, -1)
            + cyd * roll_rows(c, 1)
            + czr * roll_lanes(c, -lv.repeat)
            + czl * roll_lanes(c, lv.repeat)
        )
    return sums


def mask_planes(lv, f, w, n, wide, narrow, raw="k"):
    rows = row_of(lv.rows) + (n * lv.own_rows - 8)
    inside = (rows >= 0) & (rows < lv.own_rows * narrow)

    def one(p):
        at = w * lv.own + p - lv.first
        ok = inside & (at >= 0) & (at < lv.own * wide)
        f["k"][p] = jnp.where(ok, f[raw][p] * lv.scale, 0.0)

    planes(0, lv.planes, one)


def coefficients(lv, f, w, n, wide, narrow, lo, hi):
    rows = row_of(lv.rows) + (n * lv.own_rows - 8)
    inside = (rows >= 0) & (rows < lv.own_rows * narrow)
    lane = lane_of(lv.rows)
    last = lane >= LANES - lv.repeat
    edge = last | (lane < lv.repeat)
    f["cx"][lo - 1] = 0.5 * (f["k"][lo - 1] + f["k"][lo])

    def one(p):
        k = f["k"][p]
        cxu = 0.5 * (k + f["k"][p + 1])
        cxd = 0.5 * (k + f["k"][p - 1])
        cyu = 0.5 * (k + roll_rows(k, -1))
        cyd = roll_rows(cyu, 1)
        czr = jnp.where(last, 0.0, 0.5 * (k + roll_lanes(k, -lv.repeat)))
        czl = roll_lanes(czr, lv.repeat)
        d = MASS + (cxu + cxd + cyu + cyd + czr + czl + jnp.where(edge, 0.5 * k, 0.0))
        at = w * lv.own + p - lv.first
        ok = inside & (at >= 0) & (at < lv.own * wide)
        f["cx"][p] = cxu
        f["cyu"][p] = cyu
        f["cyd"][p] = cyd
        f["czr"][p] = czr
        f["czl"][p] = czl
        f["diag"][p] = d
        f["inv"][p] = jnp.where(ok, 1.0 / d, 0.0)

    planes(lo, hi, one)


def restrict(lv, read, mix, out):
    for j in range(lv.own // 2):
        mix[j] = read(2 * j) + read(2 * j + 1)
    half = lv.own_rows // 2
    even = lax.rem(lane_of(half) // lv.repeat, 2) == 0
    for j in range(lv.own // 2):
        x = mix[j, pl.ds(0, half, stride=2), :] + mix[j, pl.ds(1, half, stride=2), :]
        x = x + jnp.where(even, roll_lanes(x, -lv.repeat), roll_lanes(x, lv.repeat))
        out(j, 0.125 * x)


def smooth_down(lv, f, lo, hi):
    def first(p):
        hat = f["src"][p] * f["inv"][p]
        f["hat"][p] = hat
        f["upd"][p] = hat * (1.0 / THETA)

    planes(lo, hi, first)

    def second(p):
        x = f["upd"][p]
        (s,) = near_sum(lv, f, f["upd"], p, [x])
        z = f["hat"][p] + f["inv"][p] * s - x
        f["tmp"][p] = x + (KEEP1 * x + GAIN1 * z)

    planes(lo + 1, hi - 1, second)

    def third(p):
        x = f["tmp"][p]
        (s,) = near_sum(lv, f, f["tmp"], p, [x])
        z = f["hat"][p] + f["inv"][p] * s - x
        f["it"][p] = x + (KEEP2 * (x - f["upd"][p]) + GAIN2 * z)

    planes(lo + 2, hi - 2, third)


def smooth_up(lv, f, a, b, e, lo, hi):
    count = a.shape[0]

    def sweep(p, old, new, keep, gain):
        centers = [old[v, p] for v in range(count)]
        sums = near_sum(lv, f, old, p, centers)
        inv = f["inv"][p]
        for v in range(count):
            z = inv * sums[v] - centers[v]
            if v == 0:
                z = z + f["hat"][p]
            u = gain * z if keep is None else keep * e[v, p] + gain * z
            if new is not None:
                e[v, p] = u
            (b if new is None else new)[v, p] = centers[v] + u

    planes(lo + 1, hi - 1, lambda p: sweep(p, a, b, None, 1.0 / THETA), 1)
    planes(lo + 2, hi - 2, lambda p: sweep(p, b, a, KEEP1, GAIN1), 1)
    planes(lo + 3, hi - 3, lambda p: sweep(p, a, None, KEEP2, GAIN2), 1)


def solve4(m):
    small = m[1] < 0.5 * m[0]
    pick = lambda a, b: jnp.where(small, a, b)
    g = [pick(m[k + 1], m[8 + k] - m[9 + k]) for k in range(7)]
    rhs = [pick(m[k], m[8 + k]) for k in range(4)]
    rows = [[g[i + j] for j in range(4)] for i in range(4)]
    inv = []
    for i in range(4):
        piv = rows[i][i]
        good = piv > 1e-7 * g[2 * i]
        inv.append(jnp.where(good, 1.0 / jnp.where(good, piv, 1.0), 0.0))
        for r in range(i + 1, 4):
            factor = rows[i][r] * inv[i]
            rows[r] = [rows[r][j] - factor * rows[i][j] if j >= r else None for j in range(4)]
            rhs[r] = rhs[r] - factor * rhs[i]
    y = [None] * 4
    for i in (3, 2, 1, 0):
        t = rhs[i]
        for j in range(i + 1, 4):
            t = t - rows[i][j] * y[j]
        y[i] = t * inv[i]
    turned = [
        y[0] + y[1] + y[2] + y[3],
        -(y[1] + 2.0 * y[2] + 3.0 * y[3]),
        y[2] + 3.0 * y[3],
        -y[3],
    ]
    return [pick(a, b) for a, b in zip(y, turned)]


HALO_MID = [(dw, dn) for dw in (1, -1, 0, 2, -2) for dn in (0, 1, -1) if (dw, dn) != (0, 0)]
HALO_COARSE = [(dw, dn) for dw in (0, 1, -1, 2, -2, 3, -3) for dn in (1, -1, 0) if (dw, dn) != (0, 0)]
HALO_FINE = [(dw, dn) for dw in (1, -1, 0) for dn in (0, 1, -1) if (dw, dn) != (0, 0)]


def kernel(wide, narrow, names, heat, cond, out, *refs):
    s = dict(zip(names, refs))
    send_sem, recv_sem = s["send_sem"], s["recv_sem"]
    local_sem = s["local_sem"]
    w, n = lax.axis_index("wide"), lax.axis_index("narrow")
    z, q = w // 4, lax.rem(w, 4)
    stacks = wide // 4

    f0 = {k: s["f0_" + k] for k in FIELDS + ("tmp",)}
    f1 = {k: s["f1_" + k] for k in FIELDS + ("tmp",)}
    f2 = {k: s["f2_" + k] for k in FIELDS + ("tmp",) if "f2_" + k in s}

    def near(dw, dn):
        return (lax.rem(w + (dw + wide), wide), lax.rem(n + (dn + narrow), narrow))

    plane_peers = [
        (z * 4 + lax.rem(q + dq, 4), lax.rem(n + dn, narrow))
        for dn in sorted(range(narrow), key=lambda d: -min(d, narrow - d))
        for dq in (2, 3, 1, 0)
        if (dq, dn) != (0, 0)
    ]
    stack_peers = [
        (lax.rem(z + dz, stacks) * 4 + q, n)
        for dz in sorted(range(1, stacks), key=lambda d: -min(d, stacks - d))
    ]

    own_heat = pltpu.make_async_copy(heat, f0["src"].at[4:12, 8:40], local_sem.at[0])
    own_cond = pltpu.make_async_copy(cond, f0["k"].at[4:12, 8:40], local_sem.at[1])
    own_cond.start()
    own_heat.start()

    barrier = pltpu.get_barrier_semaphore()
    greeted = stack_peers + plane_peers + [near(*d) for d in HALO_COARSE]
    for peer in greeted:
        pl.semaphore_signal(barrier, inc=1, device_id=peer, device_id_type=MESH)

    used = [0]

    def send(src, dst, peer):
        i = used[0]
        used[0] += 1
        copy = pltpu.make_async_remote_copy(
            src_ref=src,
            dst_ref=dst,
            send_sem=send_sem.at[i],
            recv_sem=recv_sem.at[i],
            device_id=peer,
            device_id_type=MESH,
        )
        copy.start()
        return copy

    def send_rows(lv, ref_from, ref_to, halo, depth):
        copies = []
        for dw, dn in halo:
            a, c, b = lv.first, lv.own, lv.first - dw * lv.own
            if depth < lv.own and dw:
                a, b = (lv.first + lv.own - depth, lv.first - depth) if dw > 0 else (lv.first, lv.first + lv.own)
                c = depth
            ra, rc, rb = (8, lv.own_rows, 8) if dn == 0 else (lv.own_rows, 8, 0) if dn > 0 else (8, 8, 8 + lv.own_rows)
            copies.append(
                send(ref_from.at[a : a + c, ra : ra + rc], ref_to.at[b : b + c, rb : rb + rc], near(dw, dn))
            )
        return copies

    own_cond.wait()
    own_heat.wait()
    low4 = row_of(8) < 4
    pack, got = s["pack"], s["got"]

    def pack_plane(p):
        h, c = f0["src"][p + 4, 32:40], f0["k"][p + 4, 32:40]
        pack[0, p] = jnp.where(low4, roll_rows(h, 4), c)
        h, c = f0["src"][p + 4, 8:16], f0["k"][p + 4, 8:16]
        pack[1, p] = jnp.where(low4, c, roll_rows(h, 4))

    planes(0, 8, pack_plane)

    def put1(j, x):
        f1["raw"][MID.first + j, 8:24] = x

    restrict(FINE, lambda p: f0["k"][4 + p, 8:40], s["mix0"], put1)

    def put2(j, x):
        f2["raw"][COARSE.first + j, 8:16] = x

    restrict(MID, lambda p: f1["raw"][8 + p, 8:24], s["mix1"], put2)

    pl.semaphore_wait(barrier, len(greeted))

    first = [
        send(cond.at[4:8], f0["k"].at[0:4, 8:40], near(1, 0)),
        send(cond.at[0:4], f0["k"].at[12:16, 8:40], near(-1, 0)),
        send(heat.at[5:8], f0["src"].at[1:4, 8:40], near(1, 0)),
        send(heat.at[0:3], f0["src"].at[12:15, 8:40], near(-1, 0)),
        send(pack.at[0], got.at[0, 4:12], near(0, 1)),
        send(pack.at[1], got.at[1, 4:12], near(0, -1)),
        send(pack.at[0, 4:8], got.at[0, 0:4], near(1, 1)),
        send(pack.at[1, 4:8], got.at[1, 0:4], near(1, -1)),
        send(pack.at[0, 0:4], got.at[0, 12:16], near(-1, 1)),
        send(pack.at[1, 0:4], got.at[1, 12:16], near(-1, -1)),
    ]
    conds = send_rows(MID, f1["raw"], f1["raw"], HALO_MID, MID.own)
    conds2 = send_rows(COARSE, f2["raw"], f2["raw"], HALO_COARSE, COARSE.own)
    for c in first:
        c.wait_recv()

    def unpack(p):
        f0["k"][p, 0:8] = jnp.where(low4, 0.0, got[0, p])
        f0["k"][p, 40:48] = jnp.where(low4, got[1, p], 0.0)
        f0["src"][p, 0:8] = roll_rows(got[0, p], 4)
        f0["src"][p, 40:48] = roll_rows(got[1, p], 4)

    planes(0, 16, unpack)
    mask_planes(FINE, f0, w, n, wide, narrow)
    coefficients(FINE, f0, w, n, wide, narrow, 1, 15)
    smooth_down(FINE, f0, 1, 15)

    def residual(lv, f):
        def one(p):
            x = f["it"][p]
            (t,) = near_sum(lv, f, f["it"], p, [x])
            f["tmp"][p] = f["src"][p] + t - f["diag"][p] * x

        planes(lv.first, lv.first + lv.own, one)

    residual(FINE, f0)

    def put_src1(j, x):
        f1["src"][MID.first + j, 8:24] = x

    restrict(FINE, lambda p: f0["tmp"][4 + p, 8:40], s["mix0"], put_src1)
    srcs = send_rows(MID, f1["src"], f1["src"], HALO_MID, MID.own)
    its = send_rows(FINE, f0["it"], s["edge"], HALO_FINE, 3)
    for c in conds:
        c.wait_recv()
    mask_planes(MID, f1, w, n, wide, narrow, "raw")
    coefficients(MID, f1, w, n, wide, narrow, 1, 19)
    for c in conds2:
        c.wait_recv()
    mask_planes(COARSE, f2, w, n, wide, narrow, "raw")
    coefficients(COARSE, f2, w, n, wide, narrow, 1, 13)
    for c in srcs:
        c.wait_recv()
    smooth_down(MID, f1, 1, 19)
    residual(MID, f1)
    u, zed = s["basis"], s["zed"]

    def put_z(j, x):
        zed[COARSE.first + j, 8:16] = x * f2["inv"][COARSE.first + j, 8:16]

    restrict(MID, lambda p: f1["tmp"][8 + p, 8:24], s["mix1"], put_z)
    zs = send_rows(COARSE, zed, zed, HALO_COARSE, COARSE.own)
    for c in zs:
        c.wait_recv()

    rows2 = row_of(24) + (n * 8 - 8)
    in_rows = (rows2 >= 0) & (rows2 < 8 * narrow)

    def clean(p):
        at = w * 2 + p - 6
        u[0, p] = jnp.where(in_rows & (at >= 0) & (at < 2 * wide), zed[p], 0.0)

    planes(0, 14, clean)
    for k in range(4):
        lo, hi = (1 + k, 13 - k) if k < 3 else (6, 8)

        def one(p, k=k):
            x = u[k, p]
            (t,) = near_sum(COARSE, f2, u.at[k], p, [x])
            u[k + 1, p] = x - f2["inv"][p] * t

        planes(lo, hi, one)

    row8 = row_of(8)
    sums = [jnp.zeros((8, LANES), F32) for _ in range(16)]
    for p in (6, 7):
        d = f2["diag"][p, 8:16]
        b = [u[k, p, 8:16] for k in range(5)]
        c = [
            b[0],
            b[0] - b[1],
            b[0] - 2.0 * b[1] + b[2],
            b[0] - 3.0 * (b[1] - b[2]) - b[3],
            b[0] - 4.0 * (b[1] + b[3]) + 6.0 * b[2] + b[4],
        ]
        for at, vs in ((0, b), (8, c)):
            for k in range(8):
                sums[at + k] = sums[at + k] + vs[k // 2] * d * vs[(k + 1) // 2]
    tiles = []
    for half in (0, 8):
        m = jnp.zeros((8, LANES), F32)
        for k in range(8):
            m = jnp.where(row8 == k, jnp.sum(sums[half + k], axis=0, keepdims=True), m)
        tiles.append(jnp.sum(m, axis=1, keepdims=True))
    lane8 = lane_of(8)
    spread = jnp.where(lane8 == row8, tiles[0], 0.0) + jnp.where(lane8 == row8 + 8, tiles[1], 0.0)
    mine, all1, all2 = s["mine"], s["all1"], s["all2"]
    mine[0] = jnp.sum(spread, axis=0, keepdims=True)
    rank = q * narrow + n
    all1[rank] = mine[0]

    def send_sum(src, dst, peers, at):
        copies = []
        for i, peer in enumerate(peers):
            copy = pltpu.make_async_remote_copy(
                src_ref=src,
                dst_ref=dst,
                send_sem=s["sum_send"].at[at + i],
                recv_sem=s["sum_recv"].at[at + i],
                device_id=peer,
                device_id_type=MESH,
            )
            copy.start()
            copies.append(copy)
        return copies

    sums1 = send_sum(mine.at[0], all1.at[rank], plane_peers, 0)

    xa, xb, xe = s["mid_a"], s["mid_b"], s["mid_e"]

    def start_mid(p):
        xa[0, p] = f1["it"][p]
        for k in range(4):
            t = u[k, p // 2 + 2, 4:20]
            xa[1 + k, p, pl.ds(0, 16, stride=2), :] = t
            xa[1 + k, p, pl.ds(1, 16, stride=2), :] = t

    planes(3, 17, start_mid)
    smooth_up(MID, f1, xa, xb, xe, 3, 17)

    for c in sums1:
        c.wait_recv()
    mine[1] = jnp.sum(all1[...], axis=0)
    all2[z] = mine[1]
    sums2 = send_sum(mine.at[1], all2.at[z], stack_peers, len(plane_peers))

    for c in its:
        c.wait_recv()
    ya, yb, ye = s["fine_a"], s["fine_b"], s["fine_e"]
    edge = s["edge"]

    def own_edge(p):
        edge[p, 8:40] = f0["it"][p, 8:40]

    planes(4, 12, own_edge)

    def start_fine(p):
        for k in range(5):
            t = xb[k, p // 2 + 6, 4:28]
            ya[k, p, pl.ds(0, 24, stride=2), :] = t
            ya[k, p, pl.ds(1, 24, stride=2), :] = t
        ya[0, p] = ya[0, p] + jnp.where(f0["inv"][p] > 0.0, edge[p], 0.0)

    planes(1, 15, start_fine)
    smooth_up(FINE, f0, ya, yb, ye, 1, 15)

    for c in first + conds + conds2 + srcs + its + zs + sums1:
        c.wait_send()
    for c in sums2:
        c.wait_recv()
    total = jnp.sum(all2[...], axis=0)
    wide_total = jnp.broadcast_to(total, (8, LANES))
    ta = jnp.sum(jnp.where(lane8 == row8, wide_total, 0.0), axis=1, keepdims=True)
    tb = jnp.sum(jnp.where(lane8 == row8 + 8, wide_total, 0.0), axis=1, keepdims=True)
    ta, tb = jnp.broadcast_to(ta, (8, LANES)), jnp.broadcast_to(tb, (8, LANES))
    y = solve4([ta[k : k + 1] for k in range(8)] + [tb[k : k + 1] for k in range(8)])

    def combine(p):
        x = yb[0, p + 4, 8:40]
        for k in range(4):
            x = x + y[k] * yb[1 + k, p + 4, 8:40]
        out[p] = x

    planes(0, 8, combine)
    for c in sums2:
        c.wait_send()


def solution(mesh):
    wide, narrow = mesh.shape["wide"], mesh.shape["narrow"]

    def field(lv, *lead):
        return pltpu.VMEM((*lead, lv.planes, lv.rows, LANES), F32)

    scratch = {}
    for tag, lv in (("f0_", FINE), ("f1_", MID)):
        for k in FIELDS + ("tmp",):
            scratch[tag + k] = field(lv)
    for k in ("k", "raw", "cx", "cyu", "cyd", "czr", "czl", "inv", "diag"):
        scratch["f2_" + k] = field(COARSE)
    scratch["basis"] = field(COARSE, 5)
    scratch["zed"] = field(COARSE)
    scratch["edge"] = field(FINE)
    for k in ("a", "b", "e"):
        scratch["mid_" + k] = field(MID, 5)
        scratch["fine_" + k] = field(FINE, 5)
    scratch["pack"] = pltpu.VMEM((2, 8, 8, LANES), F32)
    scratch["got"] = pltpu.VMEM((2, 16, 8, LANES), F32)
    scratch["mix0"] = pltpu.VMEM((4, 32, LANES), F32)
    scratch["mix1"] = pltpu.VMEM((2, 16, LANES), F32)
    scratch["mine"] = pltpu.VMEM((2, 1, LANES), F32)
    scratch["all1"] = pltpu.VMEM((4 * narrow, 1, LANES), F32)
    scratch["all2"] = pltpu.VMEM((wide // 4, 1, LANES), F32)
    messages = 10 + 2 * len(HALO_MID) + 2 * len(HALO_COARSE) + len(HALO_FINE)
    scratch["send_sem"] = pltpu.SemaphoreType.DMA((messages,))
    scratch["recv_sem"] = pltpu.SemaphoreType.DMA((messages,))
    scratch["sum_send"] = pltpu.SemaphoreType.DMA((4 * narrow + wide // 4,))
    scratch["sum_recv"] = pltpu.SemaphoreType.DMA((4 * narrow + wide // 4,))
    scratch["local_sem"] = pltpu.SemaphoreType.DMA((2,))

    def body(heat, cond):
        return pl.pallas_call(
            functools.partial(kernel, wide, narrow, tuple(scratch)),
            out_shape=jax.ShapeDtypeStruct((8, 32, LANES), F32),
            in_specs=[pl.BlockSpec(memory_space=pl.ANY)] * 2,
            out_specs=pl.BlockSpec(memory_space=pltpu.VMEM),
            scratch_shapes=list(scratch.values()),
            compiler_params=pltpu.CompilerParams(
                collective_id=0, has_side_effects=True, vmem_limit_bytes=40 * 2**20
            ),
            cost_estimate=pl.CostEstimate(flops=50_000_000, bytes_accessed=400_000, transcendentals=0),
            name="vcycle",
        )(heat, cond)

    spec = P("wide", "narrow", None)
    return jax.shard_map(body, mesh=mesh, in_specs=(spec, spec), out_specs=spec, check_vma=False)
```

time: 1150 us -> 60 us (0.05); the launches traced: 1130 us -> 59.8 us
  blocking collectives: 750 us -> 0 us
  starting transfers between devices: 216 us -> 0 us
  waiting for transfers between devices: 99.8 us -> 0 us
  Pallas kernels: 0 us -> 57.3 us
  local copies, waits for them, and re-layouts: 35.9 us -> 2.47 us
  other arithmetic: 19.7 us -> 0 us
    psum x7 -> x0, blocking collectives: 750 us -> none  [body(): lax.psum(value, ('wide', 'narrow'))]
    ppermute x76 -> x0, starting transfers between devices: 216 us -> none  [the longest x38 151 us: padded_2(): lax.ppermute(lax.slice_in_dim(block, block.shape[dim] - width, None, axis...]
    ppermute x76 -> x0, waiting for transfers between devices: 99.8 us -> none  [the longest x38 99.7 us: padded_2(): lax.ppermute(lax.slice_in_dim(block, 0, width, axis=dim), axis, backward)]
    pallas_call x0 -> x1, Pallas kernels: none -> 57.3 us  [body(): pl.pallas_call(functools.partial(kernel, wide, narrow, tuple(scratch)), o...]
    reshape x5 -> x0, local copies, waits for them, and re-layouts: 29 us -> none  [the longest x3 21.4 us: restrict(): field.reshape(size_x // 2, 2, size_y // 2, 2, size_z // 2, 2)]
    reduce_sum x11 -> x0, other arithmetic: 13 us -> none  [the longest x4 8.32 us: restrict(): field.reshape(size_x // 2, 2, size_y // 2, 2, size_z // 2, 2)]
  transfers between devices with their start and end apart: 76 -> 0, of which waited for: 29 -> 0; matrix products, arithmetic and copies ran while one was open for 2% -> 0% of each run, Pallas kernels for 0% -> 0%
where the time goes in v1:
time: 60 us; the launch traced here: 59.8 us
  Pallas kernels  57.3 us (96%)
  local copies, waits for them, and re-layouts  2.47 us (4%)
    pallas_call x1, Pallas kernels, body(): pl.pallas_call(functools.partial(kernel, wide, narrow, tuple(scratch)), o...  57.3 us
    unnamed x5, local copies, waits for them, and re-layouts  2.47 us

profile of v1, /device:TPU:1, one launch (start us, length us, event | category | flops | bytes accessed | tf_op | source)
XLA Modules:
  0.0 59.8 jit_solution(14050712563353272809)
XLA Ops:
  0.0 0.0 copy-start
  0.0 0.9 %copy-done = f32[8,32,128]{2,1,0:T(8,128)S(1)} copy-done((f32[8,32,128]{2,1,0:T(8,128)S(1)}, f32[8,32,128]{2,1,0:T(8,128)}, u32[]{:S(2)}) %copy-start) | copy-done | bytes 131096
  0.9 0.0 copy-start.1
  0.9 0.9 %copy-done.1 = f32[8,32,128]{2,1,0:T(8,128)S(1)} copy-done((f32[8,32,128]{2,1,0:T(8,128)S(1)}, f32[8,32,128]{2,1,0:T(8,128)}, u32[]{:S(2)}) %copy-start.1) | copy-done | bytes 131096
  1.8 57.3 %vcycle.1 = f32[8,32,128]{2,1,0:T(8,128)S(1)} custom-call(f32[8,32,128]{2,1,0:T(8,128)S(1)} %copy-done, f32[8,32,128]{2,1,0:T(8,128)S(1)} %copy-done.1), custom_call_target="tpu_custom_call" | custom-call | flops 50000000 | bytes 400000 | tf_op jit(solution)/shard_map/vcycle/pallas_call | solution.py:529
  59.2 0.7 %copy.4 = f32[8,32,128]{2,1,0:T(8,128)} copy(f32[8,32,128]{2,1,0:T(8,128)S(1)} %vcycle.1) | data formatting | bytes 262144
Async XLA Ops:
  0.0 0.9 %copy-start = (f32[8,32,128]{2,1,0:T(8,128)S(1)}, f32[8,32,128]{2,1,0:T(8,128)}, u32[]{:S(2)}) copy-start(f32[8,32,128]{2,1,0:T(8,128)} %heat.1) | copy-start | bytes 393220
  0.9 0.9 %copy-start.1 = (f32[8,32,128]{2,1,0:T(8,128)S(1)}, f32[8,32,128]{2,1,0:T(8,128)}, u32[]{:S(2)}) copy-start(f32[8,32,128]{2,1,0:T(8,128)} %cond.1) | copy-start | bytes 393220

commit v2 on v1

v2 whole, which is shorter than its diff:
```python
import functools
import jax
import jax.numpy as jnp
from jax import lax
from jax.experimental import pallas as pl
from jax.experimental.pallas import tpu as pltpu
from jax.sharding import PartitionSpec as P

MASS = 0.002
LOW, HIGH = 0.25, 2.0
THETA = 0.5 * (HIGH + LOW)
DELTA = 0.5 * (HIGH - LOW)
SIGMA = THETA / DELTA
RHO1 = 1.0 / SIGMA
RHO2 = 1.0 / (2.0 * SIGMA - RHO1)
RHO3 = 1.0 / (2.0 * SIGMA - RHO2)
KEEP1, GAIN1 = RHO2 * RHO1, 2.0 * RHO2 / DELTA
KEEP2, GAIN2 = RHO3 * RHO2, 2.0 * RHO3 / DELTA
F32 = jnp.float32
LANES = 128
MESH = pl.DeviceIdType.MESH


class Level:
    def __init__(self, planes, first, own, rows, own_rows, repeat, scale):
        self.planes, self.first, self.own = planes, first, own
        self.rows, self.own_rows, self.repeat, self.scale = rows, own_rows, repeat, scale


FINE = Level(16, 4, 8, 48, 32, 1, 1.0)
MID = Level(20, 8, 4, 32, 16, 2, 0.25)
COARSE = Level(14, 6, 2, 24, 8, 4, 1.0 / 16.0)

FIELDS = ("k", "cx", "cyu", "cyd", "czr", "czl", "inv", "diag", "src", "hat", "upd", "it", "tmp")


def planes(lo, hi, fn, unroll=2):
    count = hi - lo
    while count % unroll:
        unroll -= 1
    if unroll == count:
        for p in range(lo, hi):
            fn(p)
        return

    def step(i, carry):
        for k in range(unroll):
            fn(lo + i * unroll + k)
        return carry

    lax.fori_loop(0, count // unroll, step, 0)


def roll_rows(x, by):
    return pltpu.roll(x, by % x.shape[0], 0)


def roll_lanes(x, by):
    return pltpu.roll(x, by % LANES, 1)


def lane_of(rows):
    return lax.broadcasted_iota(jnp.int32, (rows, LANES), 1)


def row_of(rows):
    return lax.broadcasted_iota(jnp.int32, (rows, LANES), 0)


def near_sum(lv, f, ref, p, centers):
    cxu, cxd = f["cx"][p], f["cx"][p - 1]
    cyu, cyd, czr, czl = f["cyu"][p], f["cyd"][p], f["czr"][p], f["czl"][p]
    sums = []
    for v, c in enumerate(centers):
        at = ref.at[v] if len(ref.shape) == 4 else ref
        sums.append(
            cxu * at[p + 1]
            + cxd * at[p - 1]
            + cyu * roll_rows(c, -1)
            + cyd * roll_rows(c, 1)
            + czr * roll_lanes(c, -lv.repeat)
            + czl * roll_lanes(c, lv.repeat)
        )
    return sums


def inside_rows(lv, n, narrow):
    rows = row_of(lv.rows) + (n * lv.own_rows - 8)
    return (rows >= 0) & (rows < lv.own_rows * narrow)


def inside(lv, in_rows, p, w, wide):
    at = w * lv.own + p - lv.first
    return in_rows & (at >= 0) & (at < lv.own * wide)


def pack2(lv, x, y):
    return jnp.where(lax.rem(lane_of(x.shape[0]) // (lv.repeat // 2), 2) == 0, x, y)


def unpack2(lv, xy):
    half = lv.repeat // 2
    first = lax.rem(lane_of(xy.shape[0]) // half, 2) == 0
    return jnp.where(first, xy, roll_lanes(xy, half)), jnp.where(first, roll_lanes(xy, -half), xy)


def coefficients(lv, f, in_rows, w, wide, lo, hi, unroll=2):
    lane = lane_of(lv.rows)
    last = lane >= LANES - lv.repeat
    edge = last | (lane < lv.repeat)
    f["cx"][lo - 1] = 0.5 * (f["k"][lo - 1] + f["k"][lo])

    def one(p):
        k = f["k"][p]
        cxu = 0.5 * (k + f["k"][p + 1])
        cxd = 0.5 * (k + f["k"][p - 1])
        cyu = 0.5 * (k + roll_rows(k, -1))
        cyd = roll_rows(cyu, 1)
        czr = jnp.where(last, 0.0, 0.5 * (k + roll_lanes(k, -lv.repeat)))
        czl = roll_lanes(czr, lv.repeat)
        d = MASS + (cxu + cxd + cyu + cyd + czr + czl + jnp.where(edge, 0.5 * k, 0.0))
        f["cx"][p] = cxu
        f["cyu"][p] = cyu
        f["cyd"][p] = cyd
        f["czr"][p] = czr
        f["czl"][p] = czl
        f["diag"][p] = d
        f["inv"][p] = jnp.where(inside(lv, in_rows, p, w, wide), 1.0 / d, 0.0)

    planes(lo, hi, one, unroll)


def restrict(lv, read, mix):
    for j in range(lv.own // 2):
        mix[j] = read(2 * j) + read(2 * j + 1)
    half = lv.own_rows // 2
    even = lax.rem(lane_of(half) // lv.repeat, 2) == 0
    found = []
    for j in range(lv.own // 2):
        x = mix[j, pl.ds(0, half, stride=2), :] + mix[j, pl.ds(1, half, stride=2), :]
        x = x + jnp.where(even, roll_lanes(x, -lv.repeat), roll_lanes(x, lv.repeat))
        found.append(0.125 * x)
    return found


def smooth_down(lv, f, lo, hi, unroll=2):
    def first(p):
        hat = f["src"][p] * f["inv"][p]
        f["hat"][p] = hat
        f["upd"][p] = hat * (1.0 / THETA)

    planes(lo, hi, first, unroll)

    def second(p):
        x = f["upd"][p]
        (s,) = near_sum(lv, f, f["upd"], p, [x])
        z = f["hat"][p] + f["inv"][p] * s - x
        f["tmp"][p] = x + (KEEP1 * x + GAIN1 * z)

    planes(lo + 1, hi - 1, second, unroll)

    def third(p):
        x = f["tmp"][p]
        (s,) = near_sum(lv, f, f["tmp"], p, [x])
        z = f["hat"][p] + f["inv"][p] * s - x
        f["it"][p] = x + (KEEP2 * (x - f["upd"][p]) + GAIN2 * z)

    planes(lo + 2, hi - 2, third, unroll)


def smooth_up(lv, f, a, b, e, lo, hi):
    count = a.shape[0]

    def sweep(p, old, new, keep, gain):
        centers = [old[v, p] for v in range(count)]
        sums = near_sum(lv, f, old, p, centers)
        inv = f["inv"][p]
        for v in range(count):
            z = inv * sums[v] - centers[v]
            if v == 0:
                z = z + f["hat"][p]
            u = gain * z if keep is None else keep * e[v, p] + gain * z
            if new is not None:
                e[v, p] = u
            (b if new is None else new)[v, p] = centers[v] + u

    planes(lo + 1, hi - 1, lambda p: sweep(p, a, b, None, 1.0 / THETA), 1)
    planes(lo + 2, hi - 2, lambda p: sweep(p, b, a, KEEP1, GAIN1), 1)
    planes(lo + 3, hi - 3, lambda p: sweep(p, a, None, KEEP2, GAIN2), 1)


def solve4(m):
    small = m[1] < 0.5 * m[0]
    pick = lambda a, b: jnp.where(small, a, b)
    g = [pick(m[k + 1], m[8 + k] - m[9 + k]) for k in range(7)]
    rhs = [pick(m[k], m[8 + k]) for k in range(4)]
    rows = [[g[i + j] for j in range(4)] for i in range(4)]
    inv = []
    for i in range(4):
        piv = rows[i][i]
        good = piv > 1e-7 * g[2 * i]
        inv.append(jnp.where(good, 1.0 / jnp.where(good, piv, 1.0), 0.0))
        for r in range(i + 1, 4):
            factor = rows[i][r] * inv[i]
            rows[r] = [rows[r][j] - factor * rows[i][j] if j >= r else None for j in range(4)]
            rhs[r] = rhs[r] - factor * rhs[i]
    y = [None] * 4
    for i in (3, 2, 1, 0):
        t = rhs[i]
        for j in range(i + 1, 4):
            t = t - rows[i][j] * y[j]
        y[i] = t * inv[i]
    turned = [
        y[0] + y[1] + y[2] + y[3],
        -(y[1] + 2.0 * y[2] + 3.0 * y[3]),
        y[2] + 3.0 * y[3],
        -y[3],
    ]
    return [pick(a, b) for a, b in zip(y, turned)]


def halo(reach):
    return [(dw, dn) for dw in reach for dn in (1, -1, 0) if (dw, dn) != (0, 0)]


NEAR_MID, FAR_MID = halo((1, -1, 0)), halo((2, -2))
NEAR_COARSE, FAR_COARSE = halo((1, -1, 0, 2, -2)), halo((3, -3))
HALO_FINE = halo((1, -1, 0))


def kernel(wide, narrow, names, heat, cond, out, *refs):
    s = dict(zip(names, refs))
    w, n = lax.axis_index("wide"), lax.axis_index("narrow")
    z, ylo, core = w // 4, lax.rem(w // 2, 2), lax.rem(w, 2)
    yhi, x = n // 4, lax.rem(n, 4)
    stacks = wide // 4

    f0 = {k: s["f0_" + k] for k in FIELDS}
    f1 = {k: s["f1_" + k] for k in FIELDS}
    f2 = {k: s["f2_" + k] for k in FIELDS if "f2_" + k in s}

    def near(dw, dn):
        return (lax.rem(w + (dw + wide), wide), lax.rem(n + (dn + narrow), narrow))

    def stack(dz):
        return (lax.rem(w + (4 * dz + wide), wide), n)

    def plane_peer(dx, dhi, dlo, dc):
        to = z * 4 + lax.rem(ylo + dlo, 2) * 2 + lax.rem(core + dc, 2)
        return (to, lax.rem(yhi + dhi, 2) * 4 + lax.rem(x + dx, 4))

    plane_peers = [
        plane_peer(*d)
        for d in sorted(
            [(dx, dhi, dlo, dc) for dx in range(4) for dhi in range(2) for dlo in range(2) for dc in range(2)],
            key=lambda d: -min(d[0], 4 - d[0]) - (1 if d[2] else 2 * d[1]),
        )
        if any(d)
    ]
    stack_peers = [stack(d) for d in sorted(range(1, stacks), key=lambda d: -min(d, stacks - d))]

    barrier = pltpu.get_barrier_semaphore()
    greeted = NEAR_COARSE + FAR_COARSE
    for d in greeted:
        pl.semaphore_signal(barrier, inc=1, device_id=near(*d), device_id_type=MESH)
    own_heat = pltpu.make_async_copy(heat, f0["src"].at[4:12, 8:40], s["local_sem"].at[0])
    own_cond = pltpu.make_async_copy(cond, f0["k"].at[4:12, 8:40], s["local_sem"].at[1])
    own_cond.start()
    own_heat.start()

    used = [0]
    sent = []

    def send(src, dst, peer):
        i = used[0]
        used[0] += 1
        copy = pltpu.make_async_remote_copy(
            src_ref=src,
            dst_ref=dst,
            send_sem=s["send_sem"].at[i],
            recv_sem=s["recv_sem"].at[i],
            device_id=peer,
            device_id_type=MESH,
        )
        copy.start()
        sent.append(copy)
        return copy

    def send_rows(ref_from, ref_to, first, own, own_rows, reach, depth):
        copies = []
        for dw, dn in reach:
            a, c, b = first, own, first - dw * own
            if depth < own and dw:
                a, b = (first + own - depth, first - depth) if dw > 0 else (first, first + own)
                c = depth
            ra, rc, rb = (8, own_rows, 8) if dn == 0 else (own_rows, 8, 0) if dn > 0 else (8, 8, 8 + own_rows)
            copies.append(
                send(ref_from.at[a : a + c, ra : ra + rc], ref_to.at[b : b + c, rb : rb + rc], near(dw, dn))
            )
        return copies

    def send_mid(ref, reach):
        return send_rows(ref, ref, 4, 2, 16, reach, 2)

    def send_coarse(ref, reach):
        return send_rows(ref, ref, 3, 1, 8, reach, 1)

    def arrive(copies):
        for c in copies:
            c.wait_recv()

    tokens = [s["token0"], s["token1"], s["token2"]]

    def pass_token(i):
        for way in (1, -1):
            pl.semaphore_signal(tokens[i], inc=1, device_id=stack(way * 2**i), device_id_type=MESH)

    def take_token(i):
        pl.semaphore_wait(tokens[i], 2)

    pl.semaphore_wait(barrier, len(greeted))
    first = [
        send(cond.at[4:8], f0["k"].at[0:4, 8:40], near(1, 0)),
        send(cond.at[0:4], f0["k"].at[12:16, 8:40], near(-1, 0)),
        send(heat.at[5:8], f0["src"].at[1:4, 8:40], near(1, 0)),
        send(heat.at[0:3], f0["src"].at[12:15, 8:40], near(-1, 0)),
    ]
    own_cond.wait()
    own_heat.wait()
    low4 = row_of(8) < 4
    pack, got = s["pack"], s["got"]

    def pack_plane(p):
        h, c = f0["src"][p + 4, 32:40], f0["k"][p + 4, 32:40]
        pack[0, p] = jnp.where(low4, roll_rows(h, 4), c)
        h, c = f0["src"][p + 4, 8:16], f0["k"][p + 4, 8:16]
        pack[1, p] = jnp.where(low4, c, roll_rows(h, 4))

    planes(0, 8, pack_plane, 8)
    first += [
        send(pack.at[0], got.at[0, 4:12], near(0, 1)),
        send(pack.at[1], got.at[1, 4:12], near(0, -1)),
        send(pack.at[0, 4:8], got.at[0, 0:4], near(1, 1)),
        send(pack.at[1, 4:8], got.at[1, 0:4], near(1, -1)),
        send(pack.at[0, 0:4], got.at[0, 12:16], near(-1, 1)),
        send(pack.at[1, 0:4], got.at[1, 12:16], near(-1, -1)),
    ]

    k1p, k2p, s1p, z2p = s["k1p"], s["k2p"], s["s1p"], s["z2p"]
    one_up = restrict(FINE, lambda p: f0["k"][4 + p, 8:40], s["mix0"])
    two_up = restrict(MID, lambda p: one_up[p], s["mix1"])
    for j in range(2):
        k1p[4 + j, 8:24] = pack2(MID, one_up[2 * j], one_up[2 * j + 1])
    k2p[3, 8:16] = pack2(COARSE, two_up[0], two_up[1])

    in0, in1, in2 = (inside_rows(lv, n, narrow) for lv in (FINE, MID, COARSE))

    def unpack_cond(lv, packed, f, in_rows, p):
        for k, v in enumerate(unpack2(lv, packed[p])):
            ok = inside(lv, in_rows, 2 * p + k, w, wide)
            f["k"][2 * p + k] = jnp.where(ok, v * lv.scale, 0.0)

    arrive(first)
    pass_token(0)
    cond1 = send_mid(k1p, NEAR_MID)

    def unpack(p):
        ok = inside(FINE, in0, p, w, wide)
        lo, hi = f0["k"].at[p, 0:8], f0["k"].at[p, 40:48]
        lo[...] = jnp.where(low4, 0.0, got[0, p])
        hi[...] = jnp.where(low4, got[1, p], 0.0)
        f0["src"][p, 0:8] = roll_rows(got[0, p], 4)
        f0["src"][p, 40:48] = roll_rows(got[1, p], 4)
        f0["k"][p] = jnp.where(ok, f0["k"][p], 0.0)

    planes(0, 16, unpack, 4)
    coefficients(FINE, f0, in0, w, wide, 1, 15)
    smooth_down(FINE, f0, 1, 15)

    def residual(lv, f, unroll):
        def one(p):
            x = f["it"][p]
            (t,) = near_sum(lv, f, f["it"], p, [x])
            f["tmp"][p] = f["src"][p] + t - f["diag"][p] * x

        planes(lv.first, lv.first + lv.own, one, unroll)

    residual(FINE, f0, 2)
    r1 = restrict(FINE, lambda p: f0["tmp"][4 + p, 8:40], s["mix0"])
    for j in range(2):
        s1p[4 + j, 8:24] = pack2(MID, r1[2 * j], r1[2 * j + 1])
    src1 = send_mid(s1p, NEAR_MID)
    cond2 = send_coarse(k2p, NEAR_COARSE)
    its = send_rows(f0["it"], s["edge"], 4, 8, 32, HALO_FINE, 3)
    cond1_far = send_mid(k1p, FAR_MID)
    arrive(cond1)
    for p in range(2, 8):
        unpack_cond(MID, k1p, f1, in1, p)
    coefficients(MID, f1, in1, w, wide, 5, 15, 10)
    arrive(src1)
    take_token(0)
    pass_token(1)

    def unpack_src(p):
        f1["src"][2 * p], f1["src"][2 * p + 1] = unpack2(MID, s1p[p])

    for p in range(2, 8):
        unpack_src(p)
    smooth_down(MID, f1, 5, 15, 10)
    residual(MID, f1, 4)
    r2 = restrict(MID, lambda p: f1["tmp"][8 + p, 8:24], s["mix1"])
    arrive(cond2)
    for p in range(1, 6):
        unpack_cond(COARSE, k2p, f2, in2, p)
    coefficients(COARSE, f2, in2, w, wide, 3, 11, 8)
    z2p[3, 8:16] = pack2(COARSE, r2[0] * f2["inv"][6, 8:16], r2[1] * f2["inv"][7, 8:16])
    z2 = send_coarse(z2p, NEAR_COARSE)
    z2_far = send_coarse(z2p, FAR_COARSE)
    cond2_far = send_coarse(k2p, FAR_COARSE)
    src1_far = send_mid(s1p, FAR_MID)
    arrive(z2)
    take_token(1)
    pass_token(2)
    u = s["basis"]

    def unpack_z(p):
        for k, v in enumerate(unpack2(COARSE, z2p[p])):
            u[0, 2 * p + k] = jnp.where(inside(COARSE, in2, 2 * p + k, w, wide), v, 0.0)

    def apply_b(k, p):
        v = u[k, p]
        (t,) = near_sum(COARSE, f2, u.at[k], p, [v])
        u[k + 1, p] = v - f2["inv"][p] * t

    for p in range(1, 6):
        unpack_z(p)
    for k in range(4):
        for p in range(3 + k, 11 - k):
            apply_b(k, p)

    row8, lane8 = row_of(8), lane_of(8)
    sums = [jnp.zeros((8, LANES), F32) for _ in range(16)]
    for p in (6, 7):
        d = f2["diag"][p, 8:16]
        b = [u[k, p, 8:16] for k in range(5)]
        c = [
            b[0],
            b[0] - b[1],
            b[0] - 2.0 * b[1] + b[2],
            b[0] - 3.0 * (b[1] - b[2]) - b[3],
            b[0] - 4.0 * (b[1] + b[3]) + 6.0 * b[2] + b[4],
        ]
        for at, vs in ((0, b), (8, c)):
            for k in range(8):
                sums[at + k] = sums[at + k] + vs[k // 2] * d * vs[(k + 1) // 2]
    tiles = []
    for half in (0, 8):
        m = jnp.zeros((8, LANES), F32)
        for k in range(8):
            m = jnp.where(row8 == k, jnp.sum(sums[half + k], axis=0, keepdims=True), m)
        tiles.append(jnp.sum(m, axis=1, keepdims=True))
    spread = jnp.where(lane8 == row8, tiles[0], 0.0) + jnp.where(lane8 == row8 + 8, tiles[1], 0.0)
    mine, all1, all2 = s["mine"], s["all1"], s["all2"]
    mine[0] = jnp.sum(spread, axis=0, keepdims=True)
    rank = lax.rem(w, 4) * narrow + n
    all1[rank] = mine[0]

    def send_sum(src, dst, peers, at):
        copies = []
        for i, peer in enumerate(peers):
            copy = pltpu.make_async_remote_copy(
                src_ref=src,
                dst_ref=dst,
                send_sem=s["sum_send"].at[at + i],
                recv_sem=s["sum_recv"].at[at + i],
                device_id=peer,
                device_id_type=MESH,
            )
            copy.start()
            copies.append(copy)
        return copies

    sums1 = send_sum(mine.at[0], all1.at[rank], plane_peers, 0)

    arrive(cond2_far + z2_far)
    for p in (0, 6):
        unpack_cond(COARSE, k2p, f2, in2, p)
        unpack_z(p)
    coefficients(COARSE, f2, in2, w, wide, 1, 3)
    coefficients(COARSE, f2, in2, w, wide, 11, 13)
    for k in range(3):
        for p in (1 + k, 2 + k, 11 - k, 12 - k):
            apply_b(k, p)
    arrive(cond1_far + src1_far)
    for p in (0, 1, 8, 9):
        unpack_cond(MID, k1p, f1, in1, p)
        unpack_src(p)
    coefficients(MID, f1, in1, w, wide, 1, 5, 4)
    coefficients(MID, f1, in1, w, wide, 15, 19, 4)
    smooth_down(MID, f1, 1, 19)

    xa, xb, xe = s["mid_a"], s["mid_b"], s["mid_e"]

    def start_mid(p):
        xa[0, p] = f1["it"][p]
        for k in range(4):
            t = u[k, p // 2 + 2, 4:20]
            xa[1 + k, p, pl.ds(0, 16, stride=2), :] = t
            xa[1 + k, p, pl.ds(1, 16, stride=2), :] = t

    planes(3, 17, start_mid)
    smooth_up(MID, f1, xa, xb, xe, 3, 17)

    arrive(sums1)
    mine[1] = jnp.sum(all1[...], axis=0)
    all2[z] = mine[1]
    take_token(2)
    sums2 = send_sum(mine.at[1], all2.at[z], stack_peers, len(plane_peers))

    arrive(its)
    ya, yb, ye = s["fine_a"], s["fine_b"], s["fine_e"]
    edge = s["edge"]

    def own_edge(p):
        edge[p, 8:40] = f0["it"][p, 8:40]

    planes(4, 12, own_edge)

    def start_fine(p):
        for k in range(5):
            t = xb[k, p // 2 + 6, 4:28]
            ya[k, p, pl.ds(0, 24, stride=2), :] = t
            ya[k, p, pl.ds(1, 24, stride=2), :] = t
        ya[0, p] = ya[0, p] + jnp.where(f0["inv"][p] > 0.0, edge[p], 0.0)

    planes(1, 15, start_fine)
    smooth_up(FINE, f0, ya, yb, ye, 1, 15)
    for c in sent + sums1:
        c.wait_send()
    arrive(sums2)
    total = jnp.broadcast_to(jnp.sum(all2[...], axis=0), (8, LANES))
    ta = jnp.sum(jnp.where(lane8 == row8, total, 0.0), axis=1, keepdims=True)
    tb = jnp.sum(jnp.where(lane8 == row8 + 8, total, 0.0), axis=1, keepdims=True)
    ta, tb = jnp.broadcast_to(ta, (8, LANES)), jnp.broadcast_to(tb, (8, LANES))
    y = solve4([ta[k : k + 1] for k in range(8)] + [tb[k : k + 1] for k in range(8)])

    def combine(p):
        v = yb[0, p + 4, 8:40]
        for k in range(4):
            v = v + y[k] * yb[1 + k, p + 4, 8:40]
        out[p] = v

    planes(0, 8, combine, 4)
    for c in sums2:
        c.wait_send()


def solution(mesh):
    wide, narrow = mesh.shape["wide"], mesh.shape["narrow"]

    def field(lv, *lead):
        return pltpu.VMEM((*lead, lv.planes, lv.rows, LANES), F32)

    scratch = {}
    for tag, lv in (("f0_", FINE), ("f1_", MID)):
        for k in FIELDS:
            scratch[tag + k] = field(lv)
    for k in ("k", "cx", "cyu", "cyd", "czr", "czl", "inv", "diag"):
        scratch["f2_" + k] = field(COARSE)
    scratch["basis"] = field(COARSE, 5)
    scratch["edge"] = field(FINE)
    for k in ("a", "b", "e"):
        scratch["mid_" + k] = field(MID, 5)
        scratch["fine_" + k] = field(FINE, 5)
    scratch["pack"] = pltpu.VMEM((2, 8, 8, LANES), F32)
    scratch["got"] = pltpu.VMEM((2, 16, 8, LANES), F32)
    scratch["mix0"] = pltpu.VMEM((4, 32, LANES), F32)
    scratch["mix1"] = pltpu.VMEM((2, 16, LANES), F32)
    for k in ("k1p", "s1p"):
        scratch[k] = pltpu.VMEM((10, 32, LANES), F32)
    for k in ("k2p", "z2p"):
        scratch[k] = pltpu.VMEM((7, 24, LANES), F32)
    scratch["mine"] = pltpu.VMEM((2, 1, LANES), F32)
    scratch["all1"] = pltpu.VMEM((4 * narrow, 1, LANES), F32)
    scratch["all2"] = pltpu.VMEM((wide // 4, 1, LANES), F32)
    messages = 10 + len(HALO_FINE) + 2 * len(NEAR_MID + FAR_MID + NEAR_COARSE + FAR_COARSE)
    scratch["send_sem"] = pltpu.SemaphoreType.DMA((messages,))
    scratch["recv_sem"] = pltpu.SemaphoreType.DMA((messages,))
    scratch["sum_send"] = pltpu.SemaphoreType.DMA((4 * narrow + wide // 4,))
    scratch["sum_recv"] = pltpu.SemaphoreType.DMA((4 * narrow + wide // 4,))
    scratch["local_sem"] = pltpu.SemaphoreType.DMA((2,))
    for i in range(3):
        scratch[f"token{i}"] = pltpu.SemaphoreType.REGULAR

    def body(heat, cond):
        return pl.pallas_call(
            functools.partial(kernel, wide, narrow, tuple(scratch)),
            out_shape=jax.ShapeDtypeStruct((8, 32, LANES), F32),
            in_specs=[pl.BlockSpec(memory_space=pltpu.HBM)] * 2,
            out_specs=pl.BlockSpec(memory_space=pltpu.VMEM),
            scratch_shapes=list(scratch.values()),
            compiler_params=pltpu.CompilerParams(
                collective_id=0, has_side_effects=True, vmem_limit_bytes=60 * 2**20
            ),
            cost_estimate=pl.CostEstimate(flops=50_000_000, bytes_accessed=400_000, transcendentals=0),
            name="vcycle",
        )(heat, cond)

    spec = P("wide", "narrow", None)
    return jax.shard_map(body, mesh=mesh, in_specs=(spec, spec), out_specs=spec, check_vma=False)
```

time: 60 us -> 53.5 us (0.89)
  Pallas kernels: 57.3 us -> 51.7 us
  local copies, waits for them, and re-layouts: 2.47 us -> 1.57 us
    pallas_call x1, Pallas kernels: 57.3 us -> 51.7 us  [body(): pl.pallas_call(functools.partial(kernel, wide, narrow, tuple(scratch)), o...]
    unnamed x5 -> x1, local copies, waits for them, and re-layouts: 2.47 us -> 1.57 us
where the time goes in v2:
time: 53.5 us; the launch traced here: 53.3 us
  Pallas kernels  51.7 us (97%)
  local copies, waits for them, and re-layouts  1.57 us (3%)
    pallas_call x1, Pallas kernels, body(): pl.pallas_call(functools.partial(kernel, wide, narrow, tuple(scratch)), o...  51.7 us
    unnamed x1, local copies, waits for them, and re-layouts  1.57 us

profile of v2, /device:TPU:1, one launch (start us, length us, event | category | flops | bytes accessed | tf_op | source)
XLA Modules:
  0.0 53.3 jit_solution(9904999749566253163)
XLA Ops:
  0.0 51.7 %vcycle.1 = f32[8,32,128]{2,1,0:T(8,128)} custom-call(f32[8,32,128]{2,1,0:T(8,128)} %heat.1, f32[8,32,128]{2,1,0:T(8,128)} %cond.1), custom_call_target="tpu_custom_call" | custom-call | flops 50000000 | bytes 400000 | tf_op jit(solution)/shard_map/vcycle/pallas_call | solution.py:596
  51.7 1.6 %copy.4 = f32[8,32,128]{2,1,0:T(8,128)} copy(f32[8,32,128]{2,1,0:T(8,128)} %vcycle.1) | data formatting | bytes 262144

commit v3 on v2

--- a/solution.py
+++ b/solution.py
@@ -31,7 +31,7 @@
 MID = Level(20, 8, 4, 32, 16, 2, 0.25)
 COARSE = Level(14, 6, 2, 24, 8, 4, 1.0 / 16.0)
 
-FIELDS = ("k", "cx", "cyu", "cyd", "czr", "czl", "inv", "diag", "src", "hat", "upd", "it", "tmp")
+FIELDS = ("k", "cx", "cyu", "cyd", "czr", "czl", "inv", "diag", "src", "hat", "upd", "it", "tmp", "res")
 
 
 def planes(lo, hi, fn, unroll=2):
@@ -143,13 +143,11 @@
     return found
 
 
-def smooth_down(lv, f, lo, hi, unroll=2):
+def smooth_down(lv, f, steps, unroll=2):
     def first(p):
         hat = f["src"][p] * f["inv"][p]
         f["hat"][p] = hat
         f["upd"][p] = hat * (1.0 / THETA)
-
-    planes(lo, hi, first, unroll)
 
     def second(p):
         x = f["upd"][p]
@@ -157,21 +155,21 @@
         z = f["hat"][p] + f["inv"][p] * s - x
         f["tmp"][p] = x + (KEEP1 * x + GAIN1 * z)
 
-    planes(lo + 1, hi - 1, second, unroll)
-
     def third(p):
         x = f["tmp"][p]
         (s,) = near_sum(lv, f, f["tmp"], p, [x])
         z = f["hat"][p] + f["inv"][p] * s - x
         f["it"][p] = x + (KEEP2 * (x - f["upd"][p]) + GAIN2 * z)
 
-    planes(lo + 2, hi - 2, third, unroll)
-
-
-def smooth_up(lv, f, a, b, e, lo, hi):
-    count = a.shape[0]
-
-    def sweep(p, old, new, keep, gain):
+    for step, ranges in zip((first, second, third), steps):
+        for lo, hi in ranges:
+            planes(lo, hi, step, unroll)
+
+
+def sweep_up(f, lv, old, new, e, lo, hi, keep, gain, own=None):
+    count = old.shape[0]
+
+    def one(p):
         centers = [old[v, p] for v in range(count)]
         sums = near_sum(lv, f, old, p, centers)
         inv = f["inv"][p]
@@ -180,13 +178,13 @@
             if v == 0:
                 z = z + f["hat"][p]
             u = gain * z if keep is None else keep * e[v, p] + gain * z
-            if new is not None:
+            if own is None:
                 e[v, p] = u
-            (b if new is None else new)[v, p] = centers[v] + u
-
-    planes(lo + 1, hi - 1, lambda p: sweep(p, a, b, None, 1.0 / THETA), 1)
-    planes(lo + 2, hi - 2, lambda p: sweep(p, b, a, KEEP1, GAIN1), 1)
-    planes(lo + 3, hi - 3, lambda p: sweep(p, a, None, KEEP2, GAIN2), 1)
+                new[v, p] = centers[v] + u
+            else:
+                new[v, p, own] = (centers[v] + u)[own]
+
+    planes(lo, hi, one, 1)
 
 
 def solve4(m):
@@ -260,7 +258,7 @@
     stack_peers = [stack(d) for d in sorted(range(1, stacks), key=lambda d: -min(d, stacks - d))]
 
     barrier = pltpu.get_barrier_semaphore()
-    greeted = NEAR_COARSE + FAR_COARSE
+    greeted = [(1, 1), (1, -1), (-1, 1), (-1, -1), (0, 1), (0, -1), (1, 0), (-1, 0), (4, 0), (-4, 0)]
     for d in greeted:
         pl.semaphore_signal(barrier, inc=1, device_id=near(*d), device_id_type=MESH)
     own_heat = pltpu.make_async_copy(heat, f0["src"].at[4:12, 8:40], s["local_sem"].at[0])
@@ -318,13 +316,6 @@
     def take_token(i):
         pl.semaphore_wait(tokens[i], 2)
 
-    pl.semaphore_wait(barrier, len(greeted))
-    first = [
-        send(cond.at[4:8], f0["k"].at[0:4, 8:40], near(1, 0)),
-        send(cond.at[0:4], f0["k"].at[12:16, 8:40], near(-1, 0)),
-        send(heat.at[5:8], f0["src"].at[1:4, 8:40], near(1, 0)),
-        send(heat.at[0:3], f0["src"].at[12:15, 8:40], near(-1, 0)),
-    ]
     own_cond.wait()
     own_heat.wait()
     low4 = row_of(8) < 4
@@ -337,13 +328,18 @@
         pack[1, p] = jnp.where(low4, c, roll_rows(h, 4))
 
     planes(0, 8, pack_plane, 8)
-    first += [
-        send(pack.at[0], got.at[0, 4:12], near(0, 1)),
-        send(pack.at[1], got.at[1, 4:12], near(0, -1)),
+    pl.semaphore_wait(barrier, len(greeted))
+    first = [
         send(pack.at[0, 4:8], got.at[0, 0:4], near(1, 1)),
         send(pack.at[1, 4:8], got.at[1, 0:4], near(1, -1)),
         send(pack.at[0, 0:4], got.at[0, 12:16], near(-1, 1)),
         send(pack.at[1, 0:4], got.at[1, 12:16], near(-1, -1)),
+        send(cond.at[4:8], f0["k"].at[0:4, 8:40], near(1, 0)),
+        send(cond.at[0:4], f0["k"].at[12:16, 8:40], near(-1, 0)),
+        send(pack.at[0], got.at[0, 4:12], near(0, 1)),
+        send(pack.at[1], got.at[1, 4:12], near(0, -1)),
+        send(heat.at[5:8], f0["src"].at[1:4, 8:40], near(1, 0)),
+        send(heat.at[0:3], f0["src"].at[12:15, 8:40], near(-1, 0)),
     ]
 
     k1p, k2p, s1p, z2p = s["k1p"], s["k2p"], s["s1p"], s["z2p"]
@@ -375,18 +371,20 @@
 
     planes(0, 16, unpack, 4)
     coefficients(FINE, f0, in0, w, wide, 1, 15)
-    smooth_down(FINE, f0, 1, 15)
+    smooth_down(FINE, f0, ([(1, 15)], [(2, 14)], [(3, 13)]))
 
     def residual(lv, f, unroll):
+        own = slice(8, 8 + lv.own_rows)
+
         def one(p):
             x = f["it"][p]
             (t,) = near_sum(lv, f, f["it"], p, [x])
-            f["tmp"][p] = f["src"][p] + t - f["diag"][p] * x
+            f["res"][p, own] = (f["src"][p] + t - f["diag"][p] * x)[own]
 
         planes(lv.first, lv.first + lv.own, one, unroll)
 
     residual(FINE, f0, 2)
-    r1 = restrict(FINE, lambda p: f0["tmp"][4 + p, 8:40], s["mix0"])
+    r1 = restrict(FINE, lambda p: f0["res"][4 + p, 8:40], s["mix0"])
     for j in range(2):
         s1p[4 + j, 8:24] = pack2(MID, r1[2 * j], r1[2 * j + 1])
     src1 = send_mid(s1p, NEAR_MID)
@@ -406,9 +404,9 @@
 
     for p in range(2, 8):
         unpack_src(p)
-    smooth_down(MID, f1, 5, 15, 10)
+    smooth_down(MID, f1, ([(5, 15)], [(6, 14)], [(7, 13)]), 10)
     residual(MID, f1, 4)
-    r2 = restrict(MID, lambda p: f1["tmp"][8 + p, 8:24], s["mix1"])
+    r2 = restrict(MID, lambda p: f1["res"][8 + p, 8:24], s["mix1"])
     arrive(cond2)
     for p in range(1, 6):
         unpack_cond(COARSE, k2p, f2, in2, p)
@@ -497,7 +495,9 @@
         unpack_src(p)
     coefficients(MID, f1, in1, w, wide, 1, 5, 4)
     coefficients(MID, f1, in1, w, wide, 15, 19, 4)
-    smooth_down(MID, f1, 1, 19)
+    smooth_down(
+        MID, f1, ([(1, 5), (15, 19)], [(2, 6), (14, 18)], [(3, 7), (13, 17)]), 4
+    )
 
     xa, xb, xe = s["mid_a"], s["mid_b"], s["mid_e"]
 
@@ -509,14 +509,15 @@
             xa[1 + k, p, pl.ds(1, 16, stride=2), :] = t
 
     planes(3, 17, start_mid)
-    smooth_up(MID, f1, xa, xb, xe, 3, 17)
-
+    sweep_up(f1, MID, xa, xb, xe, 4, 16, None, 1.0 / THETA)
     arrive(sums1)
     mine[1] = jnp.sum(all1[...], axis=0)
     all2[z] = mine[1]
     take_token(2)
     sums2 = send_sum(mine.at[1], all2.at[z], stack_peers, len(plane_peers))
 
+    sweep_up(f1, MID, xb, xa, xe, 5, 15, KEEP1, GAIN1)
+    sweep_up(f1, MID, xa, xb, xe, 6, 14, KEEP2, GAIN2)
     arrive(its)
     ya, yb, ye = s["fine_a"], s["fine_b"], s["fine_e"]
     edge = s["edge"]
@@ -534,7 +535,9 @@
         ya[0, p] = ya[0, p] + jnp.where(f0["inv"][p] > 0.0, edge[p], 0.0)
 
     planes(1, 15, start_fine)
-    smooth_up(FINE, f0, ya, yb, ye, 1, 15)
+    sweep_up(f0, FINE, ya, yb, ye, 2, 14, None, 1.0 / THETA)
+    sweep_up(f0, FINE, yb, ya, ye, 3, 13, KEEP1, GAIN1)
+    sweep_up(f0, FINE, ya, yb, ye, 4, 12, KEEP2, GAIN2, slice(8, 40))
     for c in sent + sums1:
         c.wait_send()
     arrive(sums2)
@@ -593,14 +596,16 @@
         scratch[f"token{i}"] = pltpu.SemaphoreType.REGULAR
 
     def body(heat, cond):
+        heat = pltpu.with_memory_space_constraint(heat, pltpu.HBM)
+        cond = pltpu.with_memory_space_constraint(cond, pltpu.HBM)
         return pl.pallas_call(
             functools.partial(kernel, wide, narrow, tuple(scratch)),
-            out_shape=jax.ShapeDtypeStruct((8, 32, LANES), F32),
+            out_shape=pltpu.VMEM((8, 32, LANES), F32),
             in_specs=[pl.BlockSpec(memory_space=pltpu.HBM)] * 2,
             out_specs=pl.BlockSpec(memory_space=pltpu.VMEM),
             scratch_shapes=list(scratch.values()),
             compiler_params=pltpu.CompilerParams(
-                collective_id=0, has_side_effects=True, vmem_limit_bytes=60 * 2**20
+                collective_id=0, has_side_effects=True, vmem_limit_bytes=40 * 2**20
             ),
             cost_estimate=pl.CostEstimate(flops=50_000_000, bytes_accessed=400_000, transcendentals=0),
             name="vcycle",

time: 53.5 us -> 49.8 us (0.931)
  Pallas kernels: 51.7 us -> 49 us
  local copies, waits for them, and re-layouts: 1.57 us -> 0.66 us
    pallas_call x1, Pallas kernels: 51.7 us -> 49 us  [body(): pl.pallas_call(functools.partial(kernel, wide, narrow, tuple(scratch)), o...]
    unnamed x1, local copies, waits for them, and re-layouts: 1.57 us -> 0.66 us
where the time goes in v3:
time: 49.8 us; the launch traced here: 49.7 us
  Pallas kernels  49 us (98%)
  local copies, waits for them, and re-layouts  0.66 us (1%)
    pallas_call x1, Pallas kernels, body(): pl.pallas_call(functools.partial(kernel, wide, narrow, tuple(scratch)), o...  49 us

profile of v3, /device:TPU:1, one launch (start us, length us, event | category | flops | bytes accessed | tf_op | source)
XLA Modules:
  0.0 49.7 jit_solution(1970920574189004893)
XLA Ops:
  0.0 49.0 %vcycle.1 = f32[8,32,128]{2,1,0:T(8,128)S(1)} custom-call(f32[8,32,128]{2,1,0:T(8,128)} %heat.1, f32[8,32,128]{2,1,0:T(8,128)} %cond.1), custom_call_target="tpu_custom_call" | custom-call | flops 50000000 | bytes 400000 | tf_op jit(solution)/shard_map/vcycle/pallas_call | solution.py:601
  49.0 0.7 %copy.4 = f32[8,32,128]{2,1,0:T(8,128)} copy(f32[8,32,128]{2,1,0:T(8,128)S(1)} %vcycle.1) | data formatting | bytes 262144

commit v4 on v3

--- a/solution.py
+++ b/solution.py
@@ -34,8 +34,9 @@
 FIELDS = ("k", "cx", "cyu", "cyd", "czr", "czl", "inv", "diag", "src", "hat", "upd", "it", "tmp", "res")
 
 
-def planes(lo, hi, fn, unroll=2):
+def planes(lo, hi, fn, unroll=99):
     count = hi - lo
+    unroll = min(unroll, count)
     while count % unroll:
         unroll -= 1
     if unroll == count:
@@ -90,6 +91,8 @@
 
 
 def inside(lv, in_rows, p, w, wide):
+    if isinstance(p, int) and lv.first <= p < lv.first + lv.own:
+        return in_rows
     at = w * lv.own + p - lv.first
     return in_rows & (at >= 0) & (at < lv.own * wide)
 
@@ -104,7 +107,7 @@
     return jnp.where(first, xy, roll_lanes(xy, half)), jnp.where(first, roll_lanes(xy, -half), xy)
 
 
-def coefficients(lv, f, in_rows, w, wide, lo, hi, unroll=2):
+def coefficients(lv, f, in_rows, w, wide, lo, hi, unroll=99):
     lane = lane_of(lv.rows)
     last = lane >= LANES - lv.repeat
     edge = last | (lane < lv.repeat)
@@ -143,7 +146,7 @@
     return found
 
 
-def smooth_down(lv, f, steps, unroll=2):
+def smooth_down(lv, f, steps, unroll=99):
     def first(p):
         hat = f["src"][p] * f["inv"][p]
         f["hat"][p] = hat
@@ -166,7 +169,7 @@
             planes(lo, hi, step, unroll)
 
 
-def sweep_up(f, lv, old, new, e, lo, hi, keep, gain, own=None):
+def sweep_up(f, lv, old, new, e, lo, hi, keep, gain, own=None, unroll=2):
     count = old.shape[0]
 
     def one(p):
@@ -184,7 +187,7 @@
             else:
                 new[v, p, own] = (centers[v] + u)[own]
 
-    planes(lo, hi, one, 1)
+    planes(lo, hi, one, unroll)
 
 
 def solve4(m):
@@ -218,7 +221,7 @@
 
 
 def halo(reach):
-    return [(dw, dn) for dw in reach for dn in (1, -1, 0) if (dw, dn) != (0, 0)]
+    return [(dw, dn) for dn in (1, -1, 0) for dw in reach if (dw, dn) != (0, 0)]
 
 
 NEAR_MID, FAR_MID = halo((1, -1, 0)), halo((2, -2))
@@ -356,21 +359,24 @@
             ok = inside(lv, in_rows, 2 * p + k, w, wide)
             f["k"][2 * p + k] = jnp.where(ok, v * lv.scale, 0.0)
 
-    arrive(first)
+    arrive(first[:8])
     pass_token(0)
     cond1 = send_mid(k1p, NEAR_MID)
 
+    in_low, in_high = in0[0:8] & ~low4, in0[40:48] & low4
+
     def unpack(p):
-        ok = inside(FINE, in0, p, w, wide)
-        lo, hi = f0["k"].at[p, 0:8], f0["k"].at[p, 40:48]
-        lo[...] = jnp.where(low4, 0.0, got[0, p])
-        hi[...] = jnp.where(low4, got[1, p], 0.0)
+        f0["k"][p, 0:8] = jnp.where(in_low, got[0, p], 0.0)
+        f0["k"][p, 40:48] = jnp.where(in_high, got[1, p], 0.0)
         f0["src"][p, 0:8] = roll_rows(got[0, p], 4)
         f0["src"][p, 40:48] = roll_rows(got[1, p], 4)
-        f0["k"][p] = jnp.where(ok, f0["k"][p], 0.0)
-
-    planes(0, 16, unpack, 4)
+        if not 4 <= p < 12:
+            at = w * 8 + p - 4
+            f0["k"][p] = jnp.where((at >= 0) & (at < 8 * wide), f0["k"][p], 0.0)
+
+    planes(0, 16, unpack)
     coefficients(FINE, f0, in0, w, wide, 1, 15)
+    arrive(first[8:])
     smooth_down(FINE, f0, ([(1, 15)], [(2, 14)], [(3, 13)]))
 
     def residual(lv, f, unroll):
@@ -383,7 +389,7 @@
 
         planes(lv.first, lv.first + lv.own, one, unroll)
 
-    residual(FINE, f0, 2)
+    residual(FINE, f0, 8)
     r1 = restrict(FINE, lambda p: f0["res"][4 + p, 8:40], s["mix0"])
     for j in range(2):
         s1p[4 + j, 8:24] = pack2(MID, r1[2 * j], r1[2 * j + 1])
@@ -463,14 +469,14 @@
     rank = lax.rem(w, 4) * narrow + n
     all1[rank] = mine[0]
 
-    def send_sum(src, dst, peers, at):
+    def send_sum(src, dst, peers, at, stage):
         copies = []
         for i, peer in enumerate(peers):
             copy = pltpu.make_async_remote_copy(
                 src_ref=src,
                 dst_ref=dst,
                 send_sem=s["sum_send"].at[at + i],
-                recv_sem=s["sum_recv"].at[at + i],
+                recv_sem=s["sum_recv"].at[stage],
                 device_id=peer,
                 device_id_type=MESH,
             )
@@ -478,7 +484,7 @@
             copies.append(copy)
         return copies
 
-    sums1 = send_sum(mine.at[0], all1.at[rank], plane_peers, 0)
+    sums1 = send_sum(mine.at[0], all1.at[rank], plane_peers, 0, 0)
 
     arrive(cond2_far + z2_far)
     for p in (0, 6):
@@ -508,13 +514,14 @@
             xa[1 + k, p, pl.ds(0, 16, stride=2), :] = t
             xa[1 + k, p, pl.ds(1, 16, stride=2), :] = t
 
-    planes(3, 17, start_mid)
+    planes(3, 17, start_mid, 2)
     sweep_up(f1, MID, xa, xb, xe, 4, 16, None, 1.0 / THETA)
-    arrive(sums1)
+    others = all1.at[pl.ds(0, len(plane_peers))]
+    pltpu.make_async_copy(others, others, s["sum_recv"].at[0]).wait()
     mine[1] = jnp.sum(all1[...], axis=0)
     all2[z] = mine[1]
     take_token(2)
-    sums2 = send_sum(mine.at[1], all2.at[z], stack_peers, len(plane_peers))
+    sums2 = send_sum(mine.at[1], all2.at[z], stack_peers, len(plane_peers), 1)
 
     sweep_up(f1, MID, xb, xa, xe, 5, 15, KEEP1, GAIN1)
     sweep_up(f1, MID, xa, xb, xe, 6, 14, KEEP2, GAIN2)
@@ -534,13 +541,14 @@
             ya[k, p, pl.ds(1, 24, stride=2), :] = t
         ya[0, p] = ya[0, p] + jnp.where(f0["inv"][p] > 0.0, edge[p], 0.0)
 
-    planes(1, 15, start_fine)
+    planes(1, 15, start_fine, 2)
     sweep_up(f0, FINE, ya, yb, ye, 2, 14, None, 1.0 / THETA)
     sweep_up(f0, FINE, yb, ya, ye, 3, 13, KEEP1, GAIN1)
     sweep_up(f0, FINE, ya, yb, ye, 4, 12, KEEP2, GAIN2, slice(8, 40))
     for c in sent + sums1:
         c.wait_send()
-    arrive(sums2)
+    others = all2.at[pl.ds(0, len(stack_peers))]
+    pltpu.make_async_copy(others, others, s["sum_recv"].at[1]).wait()
     total = jnp.broadcast_to(jnp.sum(all2[...], axis=0), (8, LANES))
     ta = jnp.sum(jnp.where(lane8 == row8, total, 0.0), axis=1, keepdims=True)
     tb = jnp.sum(jnp.where(lane8 == row8 + 8, total, 0.0), axis=1, keepdims=True)
@@ -590,7 +598,7 @@
     scratch["send_sem"] = pltpu.SemaphoreType.DMA((messages,))
     scratch["recv_sem"] = pltpu.SemaphoreType.DMA((messages,))
     scratch["sum_send"] = pltpu.SemaphoreType.DMA((4 * narrow + wide // 4,))
-    scratch["sum_recv"] = pltpu.SemaphoreType.DMA((4 * narrow + wide // 4,))
+    scratch["sum_recv"] = pltpu.SemaphoreType.DMA((2,))
     scratch["local_sem"] = pltpu.SemaphoreType.DMA((2,))
     for i in range(3):
         scratch[f"token{i}"] = pltpu.SemaphoreType.REGULAR

time: 49.8 us -> 46.8 us (0.940)
  Pallas kernels: 49 us -> 46 us
    pallas_call x1, Pallas kernels: 49 us -> 46 us  [body(): pl.pallas_call(functools.partial(kernel, wide, narrow, tuple(scratch)), o...]
where the time goes in v4:
time: 46.8 us; the launch traced here: 46.7 us
  Pallas kernels  46 us (98%)
  local copies, waits for them, and re-layouts  0.66 us (1%)
    pallas_call x1, Pallas kernels, body(): pl.pallas_call(functools.partial(kernel, wide, narrow, tuple(scratch)), o...  46 us

profile of v4, /device:TPU:1, one launch (start us, length us, event | category | flops | bytes accessed | tf_op | source)
XLA Modules:
  0.0 46.7 jit_solution(3103455781299881358)
XLA Ops:
  0.0 46.0 %vcycle.1 = f32[8,32,128]{2,1,0:T(8,128)S(1)} custom-call(f32[8,32,128]{2,1,0:T(8,128)} %heat.1, f32[8,32,128]{2,1,0:T(8,128)} %cond.1), custom_call_target="tpu_custom_call" | custom-call | flops 50000000 | bytes 400000 | tf_op jit(solution)/shard_map/vcycle/pallas_call | solution.py:609
  46.0 0.7 %copy.4 = f32[8,32,128]{2,1,0:T(8,128)} copy(f32[8,32,128]{2,1,0:T(8,128)S(1)} %vcycle.1) | data formatting | bytes 262144

commit v5 on v4

--- a/solution.py
+++ b/solution.py
@@ -261,13 +261,16 @@
     stack_peers = [stack(d) for d in sorted(range(1, stacks), key=lambda d: -min(d, stacks - d))]
 
     barrier = pltpu.get_barrier_semaphore()
-    greeted = [(1, 1), (1, -1), (-1, 1), (-1, -1), (0, 1), (0, -1), (1, 0), (-1, 0), (4, 0), (-4, 0)]
+    greeted = HALO_FINE + [d for d in NEAR_COARSE + FAR_COARSE if d not in HALO_FINE] + [(8, 0), (-8, 0), (4, 0), (-4, 0)]
     for d in greeted:
         pl.semaphore_signal(barrier, inc=1, device_id=near(*d), device_id_type=MESH)
     own_heat = pltpu.make_async_copy(heat, f0["src"].at[4:12, 8:40], s["local_sem"].at[0])
     own_cond = pltpu.make_async_copy(cond, f0["k"].at[4:12, 8:40], s["local_sem"].at[1])
     own_cond.start()
     own_heat.start()
+    share = {k: s["share_" + k] for k in ("src", "hat", "upd", "tmp", "it", "res")}
+    for ref in share.values():
+        ref[4:16] = jnp.zeros((12, 32, LANES), F32)
 
     used = [0]
     sent = []
@@ -311,10 +314,11 @@
             c.wait_recv()
 
     tokens = [s["token0"], s["token1"], s["token2"]]
+    heard = [[stack(2), stack(-2)], [stack(4), stack(-4)], [near(0, 2), near(0, -2)]]
 
     def pass_token(i):
-        for way in (1, -1):
-            pl.semaphore_signal(tokens[i], inc=1, device_id=stack(way * 2**i), device_id_type=MESH)
+        for peer in heard[i]:
+            pl.semaphore_signal(tokens[i], inc=1, device_id=peer, device_id_type=MESH)
 
     def take_token(i):
         pl.semaphore_wait(tokens[i], 2)
@@ -352,6 +356,9 @@
         k1p[4 + j, 8:24] = pack2(MID, one_up[2 * j], one_up[2 * j + 1])
     k2p[3, 8:16] = pack2(COARSE, two_up[0], two_up[1])
 
+    cond1 = send_mid(k1p, NEAR_MID)
+    cond2 = send_coarse(k2p, NEAR_COARSE + FAR_COARSE)
+    cond1_far = send_mid(k1p, FAR_MID)
     in0, in1, in2 = (inside_rows(lv, n, narrow) for lv in (FINE, MID, COARSE))
 
     def unpack_cond(lv, packed, f, in_rows, p):
@@ -361,7 +368,7 @@
 
     arrive(first[:8])
     pass_token(0)
-    cond1 = send_mid(k1p, NEAR_MID)
+    pass_token(2)
 
     in_low, in_high = in0[0:8] & ~low4, in0[40:48] & low4
 
@@ -377,6 +384,10 @@
     planes(0, 16, unpack)
     coefficients(FINE, f0, in0, w, wide, 1, 15)
     arrive(first[8:])
+    arrive(cond1)
+    for p in range(2, 8):
+        unpack_cond(MID, k1p, f1, in1, p)
+    coefficients(MID, f1, in1, w, wide, 5, 15)
     smooth_down(FINE, f0, ([(1, 15)], [(2, 14)], [(3, 13)]))
 
     def residual(lv, f, unroll):
@@ -393,38 +404,59 @@
     r1 = restrict(FINE, lambda p: f0["res"][4 + p, 8:40], s["mix0"])
     for j in range(2):
         s1p[4 + j, 8:24] = pack2(MID, r1[2 * j], r1[2 * j + 1])
+
+    for j in range(4):
+        p, own = MID.first + j, slice(8, 24)
+        hat = r1[j] * f1["inv"][p, own]
+        share["src"][p, own] = r1[j]
+        share["hat"][p, own] = hat
+        share["upd"][p, own] = hat * (1.0 / THETA)
+    sf = dict(f1, **share)
+    smooth_down(MID, sf, ([], [(7, 13)], [(6, 14)]))
+    for p in range(5, 15):
+        v = sf["it"][p]
+        (t,) = near_sum(MID, f1, sf["it"], p, [v])
+        v = sf["src"][p] + t - f1["diag"][p] * v
+        sf["res"][p] = v if 8 <= p < 12 else jnp.where(f1["inv"][p] > 0.0, v, 0.0)
+    for p in range(8, 12):
+        for tile in (slice(0, 8), slice(24, 32)):
+            sf["res"][p, tile] = jnp.where(f1["inv"][p, tile] > 0.0, sf["res"][p, tile], 0.0)
+    mix2 = s["mix2"]
+    lane16 = lax.rem(lane_of(16), 4)
+    part = []
+    for j in range(6):
+        mix2[j] = sf["res"][4 + 2 * j] + sf["res"][5 + 2 * j]
+    for j in range(6):
+        v = mix2[j, pl.ds(0, 16, stride=2), :] + mix2[j, pl.ds(1, 16, stride=2), :]
+        part.append(0.125 * (v + jnp.where(lane16 < 2, roll_lanes(v, -2), roll_lanes(v, 2))))
+    ct, cr = s["ct"], s["cr"]
+    for i in range(2):
+        a, b, c, d = part[2 * i : 2 * i + 4]
+        ct[i] = jnp.where(lane16 < 2, jnp.where(lane16 == 0, a, b), jnp.where(lane16 == 2, c, d))
+
+    def slot(dw, dn):
+        return (dw + 3) * 3 + dn + 1
+
+    parts = []
+    for dw, dn in NEAR_COARSE + FAR_COARSE:
+        to = cr.at[slot(-dw, -dn)]
+        which = pl.ds(1, 1) if dw >= 2 else pl.ds(0, 1) if dw <= -2 else pl.ds(0, 2)
+        parts.append(send(ct.at[which], to.at[which], near(dw, dn)))
     src1 = send_mid(s1p, NEAR_MID)
-    cond2 = send_coarse(k2p, NEAR_COARSE)
     its = send_rows(f0["it"], s["edge"], 4, 8, 32, HALO_FINE, 3)
-    cond1_far = send_mid(k1p, FAR_MID)
-    arrive(cond1)
-    for p in range(2, 8):
-        unpack_cond(MID, k1p, f1, in1, p)
-    coefficients(MID, f1, in1, w, wide, 5, 15, 10)
-    arrive(src1)
-    take_token(0)
-    pass_token(1)
+    src1_far = send_mid(s1p, FAR_MID)
+    arrive(cond2)
+    for p in range(7):
+        unpack_cond(COARSE, k2p, f2, in2, p)
+    coefficients(COARSE, f2, in2, w, wide, 1, 13)
 
     def unpack_src(p):
         f1["src"][2 * p], f1["src"][2 * p + 1] = unpack2(MID, s1p[p])
 
-    for p in range(2, 8):
-        unpack_src(p)
-    smooth_down(MID, f1, ([(5, 15)], [(6, 14)], [(7, 13)]), 10)
-    residual(MID, f1, 4)
-    r2 = restrict(MID, lambda p: f1["res"][8 + p, 8:24], s["mix1"])
-    arrive(cond2)
-    for p in range(1, 6):
-        unpack_cond(COARSE, k2p, f2, in2, p)
-    coefficients(COARSE, f2, in2, w, wide, 3, 11, 8)
-    z2p[3, 8:16] = pack2(COARSE, r2[0] * f2["inv"][6, 8:16], r2[1] * f2["inv"][7, 8:16])
-    z2 = send_coarse(z2p, NEAR_COARSE)
-    z2_far = send_coarse(z2p, FAR_COARSE)
-    cond2_far = send_coarse(k2p, FAR_COARSE)
-    src1_far = send_mid(s1p, FAR_MID)
-    arrive(z2)
-    take_token(1)
-    pass_token(2)
+    arrive(parts)
+    take_token(0)
+    take_token(2)
+    pass_token(1)
     u = s["basis"]
 
     def unpack_z(p):
@@ -436,13 +468,52 @@
         (t,) = near_sum(COARSE, f2, u.at[k], p, [v])
         u[k + 1, p] = v - f2["inv"][p] * t
 
-    for p in range(1, 6):
-        unpack_z(p)
+    lane8 = lane_of(8)
+    head = lax.rem(lane8, 4) < 2
+    bonds = {j: [None] * 4 for j in range(-3, 3)}
+
+    def gain_of(j, dn, v, keep=None):
+        for i in range(2):
+            x = v[8 * i : 8 * i + 8]
+            if keep is not None:
+                x = jnp.where(keep, x, 0.0)
+            at = dn + 1 + i
+            bonds[j][at] = x if bonds[j][at] is None else bonds[j][at] + x
+
+    for dn in (-1, 0, 1):
+        lo = {d: cr.at[slot(d, dn), 0] for d in (-1, 0, 1, 2, 3)}
+        hi = {d: cr.at[slot(d, dn), 1] for d in (-3, -2, -1, 0, 1)}
+        if dn == 0:
+            lo[0], hi[0] = ct.at[0], ct.at[1]
+        gain_of(-3, dn, hi[-3][...])
+        gain_of(-2, dn, hi[-2][...])
+        gain_of(-2, dn, lo[-1][...], head)
+        gain_of(-1, dn, hi[-1][...])
+        gain_of(-1, dn, lo[0][...])
+        gain_of(0, dn, lo[1][...])
+        gain_of(0, dn, hi[0][...], ~head)
+        gain_of(1, dn, lo[2][...])
+        gain_of(1, dn, hi[1][...], ~head)
+        gain_of(2, dn, lo[3][...])
+    frame = s["frame"]
+    for j in range(-2, 3):
+        for i in range(4):
+            v = jnp.where(head, bonds[j][i], bonds[j - 1][i])
+            v = v + jnp.where(head, roll_lanes(v, -2), roll_lanes(v, 2))
+            pair = unpack2(MID, v)
+            for k in range(2):
+                frame[j + 2, k, 8 * i : 8 * i + 8] = pair[k]
+    for j in range(-2, 3):
+        for k in range(2):
+            p = 6 + 2 * j + k
+            u[0, p] = roll_rows(frame[j + 2, k], -4)[0:24] * f2["inv"][p]
+    z2p[3, 8:16] = pack2(COARSE, u[0, 6, 8:16], u[0, 7, 8:16])
+    z2_far = send_coarse(z2p, FAR_COARSE)
     for k in range(4):
         for p in range(3 + k, 11 - k):
             apply_b(k, p)
 
-    row8, lane8 = row_of(8), lane_of(8)
+    row8 = row_of(8)
     sums = [jnp.zeros((8, LANES), F32) for _ in range(16)]
     for p in (6, 7):
         d = f2["diag"][p, 8:16]
@@ -486,24 +557,20 @@
 
     sums1 = send_sum(mine.at[0], all1.at[rank], plane_peers, 0, 0)
 
-    arrive(cond2_far + z2_far)
+    arrive(cond1_far + src1 + src1_far)
+    for p in (0, 1, 8, 9):
+        unpack_cond(MID, k1p, f1, in1, p)
+    for p in range(10):
+        unpack_src(p)
+    coefficients(MID, f1, in1, w, wide, 1, 5)
+    coefficients(MID, f1, in1, w, wide, 15, 19)
+    smooth_down(MID, f1, ([(1, 19)], [(2, 18)], [(3, 17)]))
+    arrive(z2_far)
     for p in (0, 6):
-        unpack_cond(COARSE, k2p, f2, in2, p)
         unpack_z(p)
-    coefficients(COARSE, f2, in2, w, wide, 1, 3)
-    coefficients(COARSE, f2, in2, w, wide, 11, 13)
     for k in range(3):
         for p in (1 + k, 2 + k, 11 - k, 12 - k):
             apply_b(k, p)
-    arrive(cond1_far + src1_far)
-    for p in (0, 1, 8, 9):
-        unpack_cond(MID, k1p, f1, in1, p)
-        unpack_src(p)
-    coefficients(MID, f1, in1, w, wide, 1, 5, 4)
-    coefficients(MID, f1, in1, w, wide, 15, 19, 4)
-    smooth_down(
-        MID, f1, ([(1, 5), (15, 19)], [(2, 6), (14, 18)], [(3, 7), (13, 17)]), 4
-    )
 
     xa, xb, xe = s["mid_a"], s["mid_b"], s["mid_e"]
 
@@ -520,7 +587,7 @@
     pltpu.make_async_copy(others, others, s["sum_recv"].at[0]).wait()
     mine[1] = jnp.sum(all1[...], axis=0)
     all2[z] = mine[1]
-    take_token(2)
+    take_token(1)
     sums2 = send_sum(mine.at[1], all2.at[z], stack_peers, len(plane_peers), 1)
 
     sweep_up(f1, MID, xb, xa, xe, 5, 15, KEEP1, GAIN1)
@@ -594,7 +661,13 @@
     scratch["mine"] = pltpu.VMEM((2, 1, LANES), F32)
     scratch["all1"] = pltpu.VMEM((4 * narrow, 1, LANES), F32)
     scratch["all2"] = pltpu.VMEM((wide // 4, 1, LANES), F32)
-    messages = 10 + len(HALO_FINE) + 2 * len(NEAR_MID + FAR_MID + NEAR_COARSE + FAR_COARSE)
+    for k in ("src", "hat", "upd", "tmp", "it", "res"):
+        scratch["share_" + k] = field(MID)
+    scratch["mix2"] = pltpu.VMEM((6, 32, LANES), F32)
+    scratch["ct"] = pltpu.VMEM((2, 16, LANES), F32)
+    scratch["cr"] = pltpu.VMEM((21, 2, 16, LANES), F32)
+    scratch["frame"] = pltpu.VMEM((5, 2, 32, LANES), F32)
+    messages = 10 + len(HALO_FINE) + 2 * len(NEAR_MID + FAR_MID + NEAR_COARSE) + 3 * len(FAR_COARSE)
     scratch["send_sem"] = pltpu.SemaphoreType.DMA((messages,))
     scratch["recv_sem"] = pltpu.SemaphoreType.DMA((messages,))
     scratch["sum_send"] = pltpu.SemaphoreType.DMA((4 * narrow + wide // 4,))

time: 46.8 us -> 47.6 us (1.017)
  Pallas kernels: 46 us -> 46.8 us
    pallas_call x1, Pallas kernels: 46 us -> 46.8 us  [body(): pl.pallas_call(functools.partial(kernel, wide, narrow, tuple(scratch)), o...]
where the time goes in v5:
time: 47.6 us; the launch traced here: 47.5 us
  Pallas kernels  46.8 us (98%)
  local copies, waits for them, and re-layouts  0.66 us (1%)
    pallas_call x1, Pallas kernels, body(): pl.pallas_call(functools.partial(kernel, wide, narrow, tuple(scratch)), o...  46.8 us

profile of v5, /device:TPU:1, one launch (start us, length us, event | category | flops | bytes accessed | tf_op | source)
XLA Modules:
  0.0 47.5 jit_solution(9898367162771063514)
XLA Ops:
  0.0 46.8 %vcycle.1 = f32[8,32,128]{2,1,0:T(8,128)S(1)} custom-call(f32[8,32,128]{2,1,0:T(8,128)} %heat.1, f32[8,32,128]{2,1,0:T(8,128)} %cond.1), custom_call_target="tpu_custom_call" | custom-call | flops 50000000 | bytes 400000 | tf_op jit(solution)/shard_map/vcycle/pallas_call | solution.py:682
  46.8 0.7 %copy.4 = f32[8,32,128]{2,1,0:T(8,128)} copy(f32[8,32,128]{2,1,0:T(8,128)S(1)} %vcycle.1) | data formatting | bytes 262144

commit v6 on v5

--- a/solution.py
+++ b/solution.py
@@ -358,7 +358,6 @@
 
     cond1 = send_mid(k1p, NEAR_MID)
     cond2 = send_coarse(k2p, NEAR_COARSE + FAR_COARSE)
-    cond1_far = send_mid(k1p, FAR_MID)
     in0, in1, in2 = (inside_rows(lv, n, narrow) for lv in (FINE, MID, COARSE))
 
     def unpack_cond(lv, packed, f, in_rows, p):
@@ -445,6 +444,7 @@
     src1 = send_mid(s1p, NEAR_MID)
     its = send_rows(f0["it"], s["edge"], 4, 8, 32, HALO_FINE, 3)
     src1_far = send_mid(s1p, FAR_MID)
+    cond1_far = send_mid(k1p, FAR_MID)
     arrive(cond2)
     for p in range(7):
         unpack_cond(COARSE, k2p, f2, in2, p)
@@ -508,7 +508,6 @@
             p = 6 + 2 * j + k
             u[0, p] = roll_rows(frame[j + 2, k], -4)[0:24] * f2["inv"][p]
     z2p[3, 8:16] = pack2(COARSE, u[0, 6, 8:16], u[0, 7, 8:16])
-    z2_far = send_coarse(z2p, FAR_COARSE)
     for k in range(4):
         for p in range(3 + k, 11 - k):
             apply_b(k, p)
@@ -556,6 +555,7 @@
         return copies
 
     sums1 = send_sum(mine.at[0], all1.at[rank], plane_peers, 0, 0)
+    z2_far = send_coarse(z2p, FAR_COARSE)
 
     arrive(cond1_far + src1 + src1_far)
     for p in (0, 1, 8, 9):
@@ -565,6 +565,12 @@
     coefficients(MID, f1, in1, w, wide, 1, 5)
     coefficients(MID, f1, in1, w, wide, 15, 19)
     smooth_down(MID, f1, ([(1, 19)], [(2, 18)], [(3, 17)]))
+    others = all1.at[pl.ds(0, len(plane_peers))]
+    pltpu.make_async_copy(others, others, s["sum_recv"].at[0]).wait()
+    mine[1] = jnp.sum(all1[...], axis=0)
+    all2[z] = mine[1]
+    take_token(1)
+    sums2 = send_sum(mine.at[1], all2.at[z], stack_peers, len(plane_peers), 1)
     arrive(z2_far)
     for p in (0, 6):
         unpack_z(p)
@@ -583,13 +589,6 @@
 
     planes(3, 17, start_mid, 2)
     sweep_up(f1, MID, xa, xb, xe, 4, 16, None, 1.0 / THETA)
-    others = all1.at[pl.ds(0, len(plane_peers))]
-    pltpu.make_async_copy(others, others, s["sum_recv"].at[0]).wait()
-    mine[1] = jnp.sum(all1[...], axis=0)
-    all2[z] = mine[1]
-    take_token(1)
-    sums2 = send_sum(mine.at[1], all2.at[z], stack_peers, len(plane_peers), 1)
-
     sweep_up(f1, MID, xb, xa, xe, 5, 15, KEEP1, GAIN1)
     sweep_up(f1, MID, xa, xb, xe, 6, 14, KEEP2, GAIN2)
     arrive(its)
@@ -628,7 +627,7 @@
             v = v + y[k] * yb[1 + k, p + 4, 8:40]
         out[p] = v
 
-    planes(0, 8, combine, 4)
+    planes(0, 8, combine)
     for c in sums2:
         c.wait_send()
 

time: 47.6 us -> 47.5 us (level)
  no operation moved by 1% of the time
where the time goes in v6:
time: 47.5 us; the launch traced here: 47.4 us
  Pallas kernels  46.7 us (98%)
  local copies, waits for them, and re-layouts  0.66 us (1%)
    pallas_call x1, Pallas kernels, body(): pl.pallas_call(functools.partial(kernel, wide, narrow, tuple(scratch)), o...  46.7 us

profile of v6, /device:TPU:1, one launch (start us, length us, event | category | flops | bytes accessed | tf_op | source)
XLA Modules:
  0.0 47.4 jit_solution(7215544861837935357)
XLA Ops:
  0.0 46.7 %vcycle.1 = f32[8,32,128]{2,1,0:T(8,128)S(1)} custom-call(f32[8,32,128]{2,1,0:T(8,128)} %heat.1, f32[8,32,128]{2,1,0:T(8,128)} %cond.1), custom_call_target="tpu_custom_call" | custom-call | flops 50000000 | bytes 400000 | tf_op jit(solution)/shard_map/vcycle/pallas_call | solution.py:681
  46.7 0.7 %copy.4 = f32[8,32,128]{2,1,0:T(8,128)} copy(f32[8,32,128]{2,1,0:T(8,128)S(1)} %vcycle.1) | data formatting | bytes 262144

commit v7 on v6

--- a/solution.py
+++ b/solution.py
@@ -169,25 +169,25 @@
             planes(lo, hi, step, unroll)
 
 
-def sweep_up(f, lv, old, new, e, lo, hi, keep, gain, own=None, unroll=2):
-    count = old.shape[0]
-
-    def one(p):
-        centers = [old[v, p] for v in range(count)]
-        sums = near_sum(lv, f, old, p, centers)
-        inv = f["inv"][p]
-        for v in range(count):
-            z = inv * sums[v] - centers[v]
-            if v == 0:
-                z = z + f["hat"][p]
-            u = gain * z if keep is None else keep * e[v, p] + gain * z
-            if own is None:
-                e[v, p] = u
-                new[v, p] = centers[v] + u
-            else:
-                new[v, p, own] = (centers[v] + u)[own]
-
-    planes(lo, hi, one, unroll)
+def sweep_up(lv, f, old, new, upd, lo, hi, keep, gain, with_source, own=None):
+    for p in range(lo, hi):
+        c = old[p]
+        (t,) = near_sum(lv, f, old, p, [c])
+        z = f["inv"][p] * t - c
+        if with_source:
+            z = z + f["hat"][p]
+        u = gain * z if keep is None else keep * upd[p] + gain * z
+        if own is None:
+            upd[p] = u
+            new[p] = c + u
+        else:
+            new[p, own] = (c + u)[own]
+
+
+def smooth_up(lv, f, a, b, upd, lo, hi, with_source, own=None):
+    sweep_up(lv, f, a, b, upd, lo + 1, hi - 1, None, 1.0 / THETA, with_source)
+    sweep_up(lv, f, b, a, upd, lo + 2, hi - 2, KEEP1, GAIN1, with_source)
+    sweep_up(lv, f, a, b, upd, lo + 3, hi - 3, KEEP2, GAIN2, with_source, own)
 
 
 def solve4(m):
@@ -565,6 +565,28 @@
     coefficients(MID, f1, in1, w, wide, 1, 5)
     coefficients(MID, f1, in1, w, wide, 15, 19)
     smooth_down(MID, f1, ([(1, 19)], [(2, 18)], [(3, 17)]))
+
+    xa, xb, xe = s["mid_a"], s["mid_b"], s["mid_e"]
+    ya, yb, ye = s["fine_a"], s["fine_b"], s["fine_e"]
+    edge = s["edge"]
+
+    def up_fine(v, with_source):
+        for p in range(1, 15):
+            t = xb[v, p // 2 + 6, 4:28]
+            ya[v, p, pl.ds(0, 24, stride=2), :] = t
+            ya[v, p, pl.ds(1, 24, stride=2), :] = t
+        if with_source:
+            for p in range(1, 15):
+                ya[v, p] = ya[v, p] + jnp.where(f0["inv"][p] > 0.0, edge[p], 0.0)
+        smooth_up(FINE, f0, ya.at[v], yb.at[v], ye.at[v], 1, 15, with_source, slice(8, 40))
+
+    arrive(its)
+    for p in range(4, 12):
+        edge[p, 8:40] = f0["it"][p, 8:40]
+    for p in range(3, 17):
+        xa[0, p] = f1["it"][p]
+    smooth_up(MID, f1, xa.at[0], xb.at[0], xe.at[0], 3, 17, True)
+    up_fine(0, True)
     others = all1.at[pl.ds(0, len(plane_peers))]
     pltpu.make_async_copy(others, others, s["sum_recv"].at[0]).wait()
     mine[1] = jnp.sum(all1[...], axis=0)
@@ -578,39 +600,17 @@
         for p in (1 + k, 2 + k, 11 - k, 12 - k):
             apply_b(k, p)
 
-    xa, xb, xe = s["mid_a"], s["mid_b"], s["mid_e"]
-
-    def start_mid(p):
-        xa[0, p] = f1["it"][p]
-        for k in range(4):
+    def up_basis(k, carry):
+        v = k + 1
+        for p in range(3, 17):
             t = u[k, p // 2 + 2, 4:20]
-            xa[1 + k, p, pl.ds(0, 16, stride=2), :] = t
-            xa[1 + k, p, pl.ds(1, 16, stride=2), :] = t
-
-    planes(3, 17, start_mid, 2)
-    sweep_up(f1, MID, xa, xb, xe, 4, 16, None, 1.0 / THETA)
-    sweep_up(f1, MID, xb, xa, xe, 5, 15, KEEP1, GAIN1)
-    sweep_up(f1, MID, xa, xb, xe, 6, 14, KEEP2, GAIN2)
-    arrive(its)
-    ya, yb, ye = s["fine_a"], s["fine_b"], s["fine_e"]
-    edge = s["edge"]
-
-    def own_edge(p):
-        edge[p, 8:40] = f0["it"][p, 8:40]
-
-    planes(4, 12, own_edge)
-
-    def start_fine(p):
-        for k in range(5):
-            t = xb[k, p // 2 + 6, 4:28]
-            ya[k, p, pl.ds(0, 24, stride=2), :] = t
-            ya[k, p, pl.ds(1, 24, stride=2), :] = t
-        ya[0, p] = ya[0, p] + jnp.where(f0["inv"][p] > 0.0, edge[p], 0.0)
-
-    planes(1, 15, start_fine, 2)
-    sweep_up(f0, FINE, ya, yb, ye, 2, 14, None, 1.0 / THETA)
-    sweep_up(f0, FINE, yb, ya, ye, 3, 13, KEEP1, GAIN1)
-    sweep_up(f0, FINE, ya, yb, ye, 4, 12, KEEP2, GAIN2, slice(8, 40))
+            xa[v, p, pl.ds(0, 16, stride=2), :] = t
+            xa[v, p, pl.ds(1, 16, stride=2), :] = t
+        smooth_up(MID, f1, xa.at[v], xb.at[v], xe.at[v], 3, 17, False)
+        up_fine(v, False)
+        return carry
+
+    lax.fori_loop(0, 4, up_basis, 0)
     for c in sent + sums1:
         c.wait_send()
     others = all2.at[pl.ds(0, len(stack_peers))]

time: 47.5 us -> 46.2 us (0.973)
  Pallas kernels: 46.7 us -> 45.4 us
    pallas_call x1, Pallas kernels: 46.7 us -> 45.4 us  [body(): pl.pallas_call(functools.partial(kernel, wide, narrow, tuple(scratch)), o...]
where the time goes in v7:
time: 46.2 us; the launch traced here: 46.1 us
  Pallas kernels  45.4 us (98%)
  local copies, waits for them, and re-layouts  0.66 us (1%)
    pallas_call x1, Pallas kernels, body(): pl.pallas_call(functools.partial(kernel, wide, narrow, tuple(scratch)), o...  45.4 us

profile of v7, /device:TPU:1, one launch (start us, length us, event | category | flops | bytes accessed | tf_op | source)
XLA Modules:
  0.0 46.1 jit_solution(18078980666347935852)
XLA Ops:
  0.0 45.4 %vcycle.1 = f32[8,32,128]{2,1,0:T(8,128)S(1)} custom-call(f32[8,32,128]{2,1,0:T(8,128)} %heat.1, f32[8,32,128]{2,1,0:T(8,128)} %cond.1), custom_call_target="tpu_custom_call" | custom-call | flops 50000000 | bytes 400000 | tf_op jit(solution)/shard_map/vcycle/pallas_call | solution.py:681
  45.4 0.7 %copy.4 = f32[8,32,128]{2,1,0:T(8,128)} copy(f32[8,32,128]{2,1,0:T(8,128)S(1)} %vcycle.1) | data formatting | bytes 262144

commit v8 on v7

--- a/solution.py
+++ b/solution.py
@@ -335,6 +335,13 @@
         pack[1, p] = jnp.where(low4, c, roll_rows(h, 4))
 
     planes(0, 8, pack_plane, 8)
+    k1p, k2p, s1p, z2p = s["k1p"], s["k2p"], s["s1p"], s["z2p"]
+    one_up = restrict(FINE, lambda p: f0["k"][4 + p, 8:40], s["mix0"])
+    two_up = restrict(MID, lambda p: one_up[p], s["mix1"])
+    for j in range(2):
+        k1p[4 + j, 8:24] = pack2(MID, one_up[2 * j], one_up[2 * j + 1])
+    k2p[3, 8:16] = pack2(COARSE, two_up[0], two_up[1])
+
     pl.semaphore_wait(barrier, len(greeted))
     first = [
         send(pack.at[0, 4:8], got.at[0, 0:4], near(1, 1)),
@@ -349,13 +356,6 @@
         send(heat.at[0:3], f0["src"].at[12:15, 8:40], near(-1, 0)),
     ]
 
-    k1p, k2p, s1p, z2p = s["k1p"], s["k2p"], s["s1p"], s["z2p"]
-    one_up = restrict(FINE, lambda p: f0["k"][4 + p, 8:40], s["mix0"])
-    two_up = restrict(MID, lambda p: one_up[p], s["mix1"])
-    for j in range(2):
-        k1p[4 + j, 8:24] = pack2(MID, one_up[2 * j], one_up[2 * j + 1])
-    k2p[3, 8:16] = pack2(COARSE, two_up[0], two_up[1])
-
     cond1 = send_mid(k1p, NEAR_MID)
     cond2 = send_coarse(k2p, NEAR_COARSE + FAR_COARSE)
     in0, in1, in2 = (inside_rows(lv, n, narrow) for lv in (FINE, MID, COARSE))
@@ -383,22 +383,22 @@
     planes(0, 16, unpack)
     coefficients(FINE, f0, in0, w, wide, 1, 15)
     arrive(first[8:])
+    smooth_down(FINE, f0, ([(1, 15)], [(2, 14)], [(3, 13)]))
+
+    def residual(lv, f, unroll):
+        own = slice(8, 8 + lv.own_rows)
+
+        def one(p):
+            x = f["it"][p]
+            (t,) = near_sum(lv, f, f["it"], p, [x])
+            f["res"][p, own] = (f["src"][p] + t - f["diag"][p] * x)[own]
+
+        planes(lv.first, lv.first + lv.own, one, unroll)
+
     arrive(cond1)
     for p in range(2, 8):
         unpack_cond(MID, k1p, f1, in1, p)
     coefficients(MID, f1, in1, w, wide, 5, 15)
-    smooth_down(FINE, f0, ([(1, 15)], [(2, 14)], [(3, 13)]))
-
-    def residual(lv, f, unroll):
-        own = slice(8, 8 + lv.own_rows)
-
-        def one(p):
-            x = f["it"][p]
-            (t,) = near_sum(lv, f, f["it"], p, [x])
-            f["res"][p, own] = (f["src"][p] + t - f["diag"][p] * x)[own]
-
-        planes(lv.first, lv.first + lv.own, one, unroll)
-
     residual(FINE, f0, 8)
     r1 = restrict(FINE, lambda p: f0["res"][4 + p, 8:40], s["mix0"])
     for j in range(2):
@@ -437,7 +437,7 @@
         return (dw + 3) * 3 + dn + 1
 
     parts = []
-    for dw, dn in NEAR_COARSE + FAR_COARSE:
+    for dw, dn in sorted(NEAR_COARSE + FAR_COARSE, key=lambda d: (-abs(d[1]), -abs(d[0]))):
         to = cr.at[slot(-dw, -dn)]
         which = pl.ds(1, 1) if dw >= 2 else pl.ds(0, 1) if dw <= -2 else pl.ds(0, 2)
         parts.append(send(ct.at[which], to.at[which], near(dw, dn)))
@@ -539,22 +539,20 @@
     rank = lax.rem(w, 4) * narrow + n
     all1[rank] = mine[0]
 
-    def send_sum(src, dst, peers, at, stage):
-        copies = []
-        for i, peer in enumerate(peers):
+    def send_sum(src, dst, peers, stage):
+        for peer in peers:
             copy = pltpu.make_async_remote_copy(
                 src_ref=src,
                 dst_ref=dst,
-                send_sem=s["sum_send"].at[at + i],
+                send_sem=s["sum_send"].at[stage],
                 recv_sem=s["sum_recv"].at[stage],
                 device_id=peer,
                 device_id_type=MESH,
             )
             copy.start()
-            copies.append(copy)
-        return copies
-
-    sums1 = send_sum(mine.at[0], all1.at[rank], plane_peers, 0, 0)
+
+    early = list(sent)
+    send_sum(mine.at[0], all1.at[rank], plane_peers, 0)
     z2_far = send_coarse(z2p, FAR_COARSE)
 
     arrive(cond1_far + src1 + src1_far)
@@ -587,12 +585,14 @@
         xa[0, p] = f1["it"][p]
     smooth_up(MID, f1, xa.at[0], xb.at[0], xe.at[0], 3, 17, True)
     up_fine(0, True)
+    for c in early:
+        c.wait_send()
     others = all1.at[pl.ds(0, len(plane_peers))]
     pltpu.make_async_copy(others, others, s["sum_recv"].at[0]).wait()
     mine[1] = jnp.sum(all1[...], axis=0)
     all2[z] = mine[1]
     take_token(1)
-    sums2 = send_sum(mine.at[1], all2.at[z], stack_peers, len(plane_peers), 1)
+    send_sum(mine.at[1], all2.at[z], stack_peers, 1)
     arrive(z2_far)
     for p in (0, 6):
         unpack_z(p)
@@ -611,8 +611,10 @@
         return carry
 
     lax.fori_loop(0, 4, up_basis, 0)
-    for c in sent + sums1:
+    for c in z2_far:
         c.wait_send()
+    others = all1.at[pl.ds(0, len(plane_peers))]
+    pltpu.make_async_copy(others, others, s["sum_send"].at[0]).wait()
     others = all2.at[pl.ds(0, len(stack_peers))]
     pltpu.make_async_copy(others, others, s["sum_recv"].at[1]).wait()
     total = jnp.broadcast_to(jnp.sum(all2[...], axis=0), (8, LANES))
@@ -628,8 +630,7 @@
         out[p] = v
 
     planes(0, 8, combine)
-    for c in sums2:
-        c.wait_send()
+    pltpu.make_async_copy(others, others, s["sum_send"].at[1]).wait()
 
 
 def solution(mesh):
@@ -669,7 +670,7 @@
     messages = 10 + len(HALO_FINE) + 2 * len(NEAR_MID + FAR_MID + NEAR_COARSE) + 3 * len(FAR_COARSE)
     scratch["send_sem"] = pltpu.SemaphoreType.DMA((messages,))
     scratch["recv_sem"] = pltpu.SemaphoreType.DMA((messages,))
-    scratch["sum_send"] = pltpu.SemaphoreType.DMA((4 * narrow + wide // 4,))
+    scratch["sum_send"] = pltpu.SemaphoreType.DMA((2,))
     scratch["sum_recv"] = pltpu.SemaphoreType.DMA((2,))
     scratch["local_sem"] = pltpu.SemaphoreType.DMA((2,))
     for i in range(3):

time: 46.2 us -> 45.4 us (0.983)
  Pallas kernels: 45.4 us -> 44.6 us
    pallas_call x1, Pallas kernels: 45.4 us -> 44.6 us  [body(): pl.pallas_call(functools.partial(kernel, wide, narrow, tuple(scratch)), o...]
where the time goes in v8:
time: 45.4 us; the launch traced here: 45.3 us
  Pallas kernels  44.6 us (98%)
  local copies, waits for them, and re-layouts  0.66 us (1%)
    pallas_call x1, Pallas kernels, body(): pl.pallas_call(functools.partial(kernel, wide, narrow, tuple(scratch)), o...  44.6 us

profile of v8, /device:TPU:1, one launch (start us, length us, event | category | flops | bytes accessed | tf_op | source)
XLA Modules:
  0.0 45.3 jit_solution(17990640405340739239)
XLA Ops:
  0.0 44.6 %vcycle.1 = f32[8,32,128]{2,1,0:T(8,128)S(1)} custom-call(f32[8,32,128]{2,1,0:T(8,128)} %heat.1, f32[8,32,128]{2,1,0:T(8,128)} %cond.1), custom_call_target="tpu_custom_call" | custom-call | flops 50000000 | bytes 400000 | tf_op jit(solution)/shard_map/vcycle/pallas_call | solution.py:682
  44.6 0.7 %copy.4 = f32[8,32,128]{2,1,0:T(8,128)} copy(f32[8,32,128]{2,1,0:T(8,128)S(1)} %vcycle.1) | data formatting | bytes 262144

commit v9 on v8

--- a/solution.py
+++ b/solution.py
@@ -262,12 +262,14 @@
 
     barrier = pltpu.get_barrier_semaphore()
     greeted = HALO_FINE + [d for d in NEAR_COARSE + FAR_COARSE if d not in HALO_FINE] + [(8, 0), (-8, 0), (4, 0), (-4, 0)]
-    for d in greeted:
+    for d in greeted[:8]:
         pl.semaphore_signal(barrier, inc=1, device_id=near(*d), device_id_type=MESH)
     own_heat = pltpu.make_async_copy(heat, f0["src"].at[4:12, 8:40], s["local_sem"].at[0])
     own_cond = pltpu.make_async_copy(cond, f0["k"].at[4:12, 8:40], s["local_sem"].at[1])
     own_cond.start()
     own_heat.start()
+    for d in greeted[8:]:
+        pl.semaphore_signal(barrier, inc=1, device_id=near(*d), device_id_type=MESH)
     share = {k: s["share_" + k] for k in ("src", "hat", "upd", "tmp", "it", "res")}
     for ref in share.values():
         ref[4:16] = jnp.zeros((12, 32, LANES), F32)

time: 45.4 us -> 45.4 us (level)
  no operation moved by 1% of the time
where the time goes in v9:
time: 45.4 us; the launch traced here: 45.3 us
  Pallas kernels  44.6 us (98%)
  local copies, waits for them, and re-layouts  0.66 us (1%)
    pallas_call x1, Pallas kernels, body(): pl.pallas_call(functools.partial(kernel, wide, narrow, tuple(scratch)), o...  44.6 us

profile of v9, /device:TPU:1, one launch (start us, length us, event | category | flops | bytes accessed | tf_op | source)
XLA Modules:
  0.0 45.3 jit_solution(14872195305552113033)
XLA Ops:
  0.0 44.6 %vcycle.1 = f32[8,32,128]{2,1,0:T(8,128)S(1)} custom-call(f32[8,32,128]{2,1,0:T(8,128)} %heat.1, f32[8,32,128]{2,1,0:T(8,128)} %cond.1), custom_call_target="tpu_custom_call" | custom-call | flops 50000000 | bytes 400000 | tf_op jit(solution)/shard_map/vcycle/pallas_call | solution.py:684
  44.6 0.7 %copy.4 = f32[8,32,128]{2,1,0:T(8,128)} copy(f32[8,32,128]{2,1,0:T(8,128)S(1)} %vcycle.1) | data formatting | bytes 262144
